TPU v7x, 512 devices: a whole 4x4x16 slice. The times are simulated.
512 devices in a mesh: hi: 4 (over z_hi, core), lo: 128 (over y, z_lo, x).
Axes of the slice: x: 4, y: 4, z: 16 (z_hi: 2, z_lo: 8; z = z_hi * 8 + z_lo), core: 2. Of those that a mesh axis runs over, the one named last changes fastest.
Arguments:
- state: float32 [2, 2048, 128, 128], P(None, ('hi', 'lo')), may hold values from -6 to 6
- low_gates: float32 [2, 2, 128, 128], replicated, may hold values from -0.375 to 0.375
- low_order: int32 [2, 7], replicated, may hold values from 0 to 6, each once within a row
- high_gates: float32 [2, 2, 2, 2], replicated, may hold values from -3 to 3
- mid_gate: float32 [2, 128, 128], replicated, may hold values from -0.375 to 0.375
- mid_order: int32 [7], replicated, may hold values from 0 to 6, each once
Outputs:
- final_state: float32 [2, 2048, 128, 128], P(None, ('hi', 'lo'))
Inputs may be any that keep to these rules, and one draw needn't show every extreme that they name: `low_order`: each row is an order of the 7 low qubits, each once. `mid_order`: an order of the 7 qubits, each once.
All inputs are finite; a program needn't handle non-finite values.
Results may differ from a plain program's by a relative error of at most 0.000082.
Values sent between devices are 32-bit elements; how exact they have to be, the bound alone decides.
No kernel may reach another device: no remote copies, remote signals or barrier semaphores. Data moves between devices by JAX's collectives and lax.ppermute only.
A program may use at most 64 MiB of HBM per device.

v0:
```python
import jax
import jax.numpy as jnp
from jax import lax
from jax.sharding import PartitionSpec as P


def partner_2(block, axis, apart):
    count = lax.axis_size(axis)
    route = []
    for low in range(count):
        high = low | 1 << apart
        if high != low and high < count:
            route += [(low, high), (high, low)]
    return lax.ppermute(block, axis, route)


def index_map(order):
    count = order.shape[0]
    values = jnp.arange(2**count, dtype=jnp.int32)
    places = jnp.arange(count, dtype=jnp.int32)
    bits = values[:, None] >> places[None, :] & 1
    return jnp.sum(bits << order[None, :], axis=1)


def permuted(gate, order):
    where = index_map(order)
    return gate[:, where][:, :, where]


def apply_last(real, imag, matrix):

    def prod(left, right):
        return jnp.einsum("...b,ab->...a", left, right, precision=lax.Precision.HIGHEST)

    return (
        prod(real, matrix[0]) - prod(imag, matrix[1]),
        prod(real, matrix[1]) + prod(imag, matrix[0]),
    )


def apply_middle(block, matrix):

    def prod(left, right):
        return jnp.einsum("sbl,ab->sal", left, right, precision=lax.Precision.HIGHEST)

    real = prod(block[0], matrix[0]) - prod(block[1], matrix[1])
    imag = prod(block[0], matrix[1]) + prod(block[1], matrix[0])
    return jnp.stack([real, imag])


def combine(self_re, self_im, other_re, other_im, coef_self, coef_other):
    real = (
        coef_self[0] * self_re
        - coef_self[1] * self_im
        + (coef_other[0] * other_re - coef_other[1] * other_im)
    )
    imag = (
        coef_self[0] * self_im
        + coef_self[1] * self_re
        + (coef_other[0] * other_im + coef_other[1] * other_re)
    )
    return jnp.stack([real, imag])


def body(state, low_gates, low_order, high_gates, mid_gate, mid_order):
    first_matrix = permuted(low_gates[0], low_order[0])
    second_matrix = permuted(low_gates[1], low_order[1])
    mid_matrix = permuted(mid_gate, mid_order)
    real, imag = apply_last(state[0], state[1], first_matrix)
    current = jnp.stack([real, imag])
    for qubit in range(2):
        level = lax.axis_index("hi") >> qubit & 1
        partner = partner_2(current, "hi", qubit)
        unit = high_gates[qubit]
        coef_self = unit[:, level, level]
        coef_other = unit[:, level, 1 - level]
        current = combine(current[0], current[1], partner[0], partner[1], coef_self, coef_other)
    moved = lax.all_to_all(current, "lo", split_axis=2, concat_axis=2, tiled=True)
    mixed = apply_middle(moved, mid_matrix)
    current = lax.all_to_all(mixed, "lo", split_axis=2, concat_axis=2, tiled=True)
    real, imag = apply_last(current[0], current[1], second_matrix)
    return jnp.stack([real, imag])


def solution(mesh):
    return jax.shard_map(
        body,
        mesh=mesh,
        in_specs=(P(None, ("hi", "lo"), None, None), P(), P(), P(), P(), P()),
        out_specs=P(None, ("hi", "lo"), None, None),
        check_vma=False,
    )
```

profile of v0, /device:TPU:1, one launch (start us, length us, event | category | flops | bytes accessed | tf_op | source)
XLA Modules:
  0.0 166.7 jit_solution(10343273217983145118)
XLA Ops:
  0.0 0.0 copy-start
  0.0 0.0 copy-start.3
  0.0 1.0 fusion.27
  1.0 0.0 copy-done.3
  1.1 0.1 shift-left_reduce_fusion
  1.2 0.2 copy_bitcast_fusion.12
  1.4 0.0 copy-start.1
  1.4 0.7 gather_fusion.2
  2.1 0.1 copy.40
  2.3 0.8 gather_fusion.3
  3.0 0.1 copy.41
  3.1 0.0 copy-done.1
  3.1 0.4 fusion.10
  3.5 0.4 fusion.12
  3.9 0.4 convolution_add_fusion.2
  4.3 0.4 convolution_subtract_fusion.2
  4.7 8.8 %collective-permute-start = (f32[2,4,128,128]{2,3,1,0:T(8,128)S(1)}, f32[2,4,128,128]{2,3,1,0:T(8,128)S(1)}, u32[]{:S(2)}, u32[]{:S(2)}) collective-permute-start(f32[2,4,128,128]{2,3,1,0:T(8,128)S(1)} %pad_maximum_fusion), channel_id=1, source_target_pairs={{0,128},{128,0},{256,384},{384,256},{1,129},{129,1},{257,385},{385... | collective-permute-start | bytes 1572872 | tf_op jit(solution)/shard_map/ppermute | solution.py:14
  13.5 0.0 copy-start.2
  13.5 0.7 copy-done.2
  14.2 0.7 constant_dynamic-slice_fusion.2
  14.9 0.1 collective-permute-done
  15.0 2.6 %bitcast_add_fusion.2 = (f32[4,128,128]{1,2,0:T(8,128)S(1)}, f32[4,128,128]{1,2,0:T(8,128)S(1)}) fusion(f32[128,4,128]{2,0,1:T(8,128)S(1)} %convolution_add_fusion.2, f32[128,4,128]{2,0,1:T(8,128)S(1)} %convolution_subtract_fusion.2, f32[2,4,128,128]{2,3,1,0:T(8,128)S(1)} %collective-permute-done, f32[]{:T(128)} %bitcast.26, f32[]{:T(128)} %bitcast.23, ...), kind=kLoop, calls=%fused_computation.29 | loop fusion | flops 917504 | bytes 1572880 | tf_op jit(solution)/shard_map/add | solution.py:58
  17.7 10.1 %collective-permute-start.1 = (f32[2,4,128,128]{2,3,1,0:T(8,128)S(1)}, f32[2,4,128,128]{2,3,1,0:T(8,128)S(1)}, u32[]{:S(2)}, u32[]{:S(2)}) collective-permute-start(f32[2,4,128,128]{2,3,1,0:T(8,128)S(1)} %pad_maximum_fusion.1), channel_id=1, source_target_pairs={{0,256},{256,0},{128,384},{384,128},{1,257},{257,1},{129,385},{385... | collective-permute-start | bytes 1572872 | tf_op jit(solution)/shard_map/ppermute | solution.py:14
  27.7 26.4 %collective-permute-done.1 = f32[2,4,128,128]{2,3,1,0:T(8,128)S(1)} collective-permute-done((f32[2,4,128,128]{2,3,1,0:T(8,128)S(1)}, f32[2,4,128,128]{2,3,1,0:T(8,128)S(1)}, u32[]{:S(2)}, u32[]{:S(2)}) %collective-permute-start.1) | collective-permute-done | bytes 524320 | tf_op jit(solution)/shard_map/ppermute | solution.py:14
  54.1 2.6 %fusion.5 = (f32[1,4,128,128]{2,3,1,0:T(8,128)S(1)}, f32[1,4,128,128]{2,3,1,0:T(8,128)S(1)}) fusion(f32[4,128,128]{1,2,0:T(8,128)S(1)} %get-tuple-element.7, f32[4,128,128]{1,2,0:T(8,128)S(1)} %get-tuple-element.8, f32[2,4,128,128]{2,3,1,0:T(8,128)S(1)} %collective-permute-done.1, f32[]{:T(128)} %bitcast.33, f32[]{:T(128)} %bitcast.30, f32[]{:T(128)} %bitcast.28, ...), kind=kLoop, calls=%fused_computation.28 | loop fusion | flops 917504 | bytes 1572880 | tf_op jit(solution)/shard_map/stack | solution.py:62
  56.8 1.0 copy.42
  57.8 0.0 copy-start.4
  57.8 33.8 %all-to-all-start = ((f32[2,4,128,128]{3,1,0,2:T(4,128)}), f32[2,4,128,128]{3,1,0,2:T(4,128)S(1)}, u32[]{:S(2)}, u32[]{:S(2)}) async-start(f32[2,4,128,128]{3,1,0,2:T(4,128)} %copy.42), calls=%async_computation | async-start | bytes 1048576 | tf_op jit(solution)/shard_map/all_to_all | solution.py:78
  91.6 0.0 copy-done.4
  91.6 0.1 shift-left_reduce_fusion.2
  91.7 0.0 copy-done
  91.7 0.7 gather_fusion
  92.5 0.1 copy.37
  92.6 0.7 gather_fusion.1
  93.4 0.1 copy.38
  93.5 29.0 %all-to-all-done = f32[2,4,128,128]{3,1,0,2:T(4,128)S(1)} async-done(((f32[2,4,128,128]{3,1,0,2:T(4,128)}), f32[2,4,128,128]{3,1,0,2:T(4,128)S(1)}, u32[]{:S(2)}, u32[]{:S(2)}) %all-to-all-start) | async-done | bytes 524320 | tf_op jit(solution)/shard_map/all_to_all | solution.py:78
  122.5 0.1 fusion.26
  122.6 0.4 fusion.14
  123.0 0.4 fusion.15
  123.3 0.4 fusion.2
  123.7 0.4 fusion.3
  124.1 0.1 pad_maximum_fusion.3
  124.1 1.1 copy.45
  125.3 8.0 %all-to-all-start.1 = ((f32[2,4,128,128]{3,1,0,2:T(4,128)}), f32[2,4,128,128]{3,1,0,2:T(4,128)S(1)}, u32[]{:S(2)}, u32[]{:S(2)}) async-start(f32[2,4,128,128]{3,1,0,2:T(4,128)} %copy.45), calls=%async_computation.1 | async-start | bytes 1048576 | tf_op jit(solution)/shard_map/all_to_all | solution.py:80
  133.3 0.7 gather_fusion.4
  134.1 0.1 copy.48
  134.2 0.7 gather_fusion.5
  135.0 0.1 copy.49
  135.1 29.1 %all-to-all-done.1 = f32[2,4,128,128]{3,1,0,2:T(4,128)S(1)} async-done(((f32[2,4,128,128]{3,1,0,2:T(4,128)}), f32[2,4,128,128]{3,1,0,2:T(4,128)S(1)}, u32[]{:S(2)}, u32[]{:S(2)}) %all-to-all-start.1) | async-done | bytes 524320 | tf_op jit(solution)/shard_map/all_to_all | solution.py:80
  164.2 0.1 fusion.25
  164.3 0.4 fusion.16
  164.7 0.4 fusion.17
  165.0 0.4 fusion
  165.4 0.4 fusion.1
  165.8 0.8 pad_maximum_fusion.4
  (11 shorter events, 0.2 us)
Async XLA Ops:
  0.0 91.7 %copy-start = (f32[2,128,128]{2,1,0:T(8,128)S(1)}, f32[2,128,128]{2,1,0:T(8,128)}, u32[]{:S(2)}) copy-start(f32[2,128,128]{2,1,0:T(8,128)} %param.10) | copy-start | bytes 393220
  0.0 1.0 copy-start.3
  1.4 1.7 %copy-start.1 = (f32[2,4,128,128]{3,2,1,0:T(8,128)S(1)}, f32[2,4,128,128]{3,2,1,0:T(8,128)}, u32[]{:S(2)}) copy-start(f32[2,4,128,128]{3,2,1,0:T(8,128)} %param.6) | copy-start | bytes 1572868
  4.7 10.3 %collective-permute-start = (f32[2,4,128,128]{2,3,1,0:T(8,128)S(1)}, f32[2,4,128,128]{2,3,1,0:T(8,128)S(1)}, u32[]{:S(2)}, u32[]{:S(2)}) collective-permute-start(f32[2,4,128,128]{2,3,1,0:T(8,128)S(1)} %pad_maximum_fusion), channel_id=1, source_target_pairs={{0,128},{128,0},{256,384},{384,256},{1,129},{129,1},{257,385},{385... | collective-permute-start | bytes 1572872 | tf_op jit(solution)/shard_map/ppermute | solution.py:14
  13.5 0.7 copy-start.2
  17.7 36.5 %collective-permute-start.1 = (f32[2,4,128,128]{2,3,1,0:T(8,128)S(1)}, f32[2,4,128,128]{2,3,1,0:T(8,128)S(1)}, u32[]{:S(2)}, u32[]{:S(2)}) collective-permute-start(f32[2,4,128,128]{2,3,1,0:T(8,128)S(1)} %pad_maximum_fusion.1), channel_id=1, source_target_pairs={{0,256},{256,0},{128,384},{384,128},{1,257},{257,1},{129,385},{385... | collective-permute-start | bytes 1572872 | tf_op jit(solution)/shard_map/ppermute | solution.py:14
  57.8 33.8 %copy-start.4 = (s32[7]{0:T(128)S(1)}, s32[7]{0:T(128)}, u32[]{:S(2)}) copy-start(s32[7]{0:T(128)} %param.11) | copy-start | bytes 88
  57.8 64.7 %all-to-all-start = ((f32[2,4,128,128]{3,1,0,2:T(4,128)}), f32[2,4,128,128]{3,1,0,2:T(4,128)S(1)}, u32[]{:S(2)}, u32[]{:S(2)}) async-start(f32[2,4,128,128]{3,1,0,2:T(4,128)} %copy.42), calls=%async_computation | async-start | bytes 1048576 | tf_op jit(solution)/shard_map/all_to_all | solution.py:78
  125.3 38.9 %all-to-all-start.1 = ((f32[2,4,128,128]{3,1,0,2:T(4,128)}), f32[2,4,128,128]{3,1,0,2:T(4,128)S(1)}, u32[]{:S(2)}, u32[]{:S(2)}) async-start(f32[2,4,128,128]{3,1,0,2:T(4,128)} %copy.45), calls=%async_computation.1 | async-start | bytes 1048576 | tf_op jit(solution)/shard_map/all_to_all | solution.py:80
where the time goes:
time: 167 us
  waiting for transfers between devices  84.7 us (51%)
  starting transfers between devices  60.7 us (36%)
  local copies, waits for them, and re-layouts  10.1 us (6%)
  other arithmetic  6.42 us (4%)
  matrix products  4.48 us (3%)
    all_to_all x1, starting transfers between devices, body(): lax.all_to_all(current, 'lo', split_axis=2, concat_axis=2, tiled=True)  33.8 us
    all_to_all x1, waiting for transfers between devices, body(): lax.all_to_all(mixed, 'lo', split_axis=2, concat_axis=2, tiled=True)  29.1 us
    all_to_all x1, waiting for transfers between devices, body(): lax.all_to_all(current, 'lo', split_axis=2, concat_axis=2, tiled=True)  29 us
    ppermute x2, waiting for transfers between devices, partner_2(): return lax.ppermute(block, axis, route)  26.5 us
    ppermute x2, starting transfers between devices, partner_2(): return lax.ppermute(block, axis, route)  18.9 us
    all_to_all x1, starting transfers between devices, body(): lax.all_to_all(mixed, 'lo', split_axis=2, concat_axis=2, tiled=True)  8.02 us
    gather x12, local copies, waits for them, and re-layouts, permuted(): return gate[:, where][:, :, where]  5.11 us
  transfers between devices with their start and end apart: 4, of which 4 were waited for; matrix products, arithmetic and copies ran while one was open for 3% of the time, Pallas kernels for 0%

commit v1 on v0

v1 whole, which is shorter than its diff:
```python
import jax
import jax.numpy as jnp
from jax import lax
from jax.sharding import PartitionSpec as P

AXES = ("hi", "lo")
HIGHEST = lax.Precision.HIGHEST


def index_map(order):
    count = order.shape[0]
    values = jnp.arange(2**count, dtype=jnp.int32)
    places = jnp.arange(count, dtype=jnp.int32)
    bits = values[:, None] >> places[None, :] & 1
    return jnp.sum(bits << order[None, :], axis=1)


def permuted(gate, order):
    where = index_map(order)
    pick = (where[:, None] == jnp.arange(gate.shape[-1])[None, :]).astype(gate.dtype)
    half = jnp.einsum("ai,cij->caj", pick, gate, precision=HIGHEST)
    return jnp.einsum("caj,bj->cab", half, pick, precision=HIGHEST)


def product(left, right):
    def prod(a, b):
        return jnp.dot(a, b, precision=HIGHEST)

    return jnp.stack(
        [
            prod(left[0], right[0]) - prod(left[1], right[1]),
            prod(left[0], right[1]) + prod(left[1], right[0]),
        ]
    )


def combine(mine, other, unit, level):
    own, cross = unit[:, level, level], unit[:, level, 1 - level]
    return (
        own[0] * mine[0] - own[1] * mine[1] + (cross[0] * other[0] - cross[1] * other[1]),
        own[0] * mine[1] + own[1] * mine[0] + (cross[0] * other[1] + cross[1] * other[0]),
    )


def high(parts, high_gates):
    for qubit in range(2):
        parts = [
            combine(parts[h], parts[h ^ 1 << qubit], high_gates[qubit], h >> qubit & 1)
            for h in range(4)
        ]
    return parts


def body(state, low_gates, low_order, high_gates, mid_gate, mid_order):
    rows, order = state.shape[1], state.shape[3]
    peers = rows * state.shape[2]
    low = product(permuted(low_gates[1], low_order[1]), permuted(low_gates[0], low_order[0]))
    mid = permuted(mid_gate, mid_order)
    sent = jnp.transpose(state, (1, 2, 0, 3)).reshape(peers, 2, order)
    moved = lax.all_to_all(sent, AXES, 0, 0, tiled=True)
    group = moved.reshape(4, -1, 2, order)
    parts = high([(group[h, :, 0], group[h, :, 1]) for h in range(4)], high_gates)
    stacked = jnp.concatenate(
        [jnp.concatenate([re, im], axis=0) for re, im in parts], axis=1
    )
    mid_real = jnp.concatenate(
        [jnp.concatenate([mid[0], -mid[1]], 1), jnp.concatenate([mid[1], mid[0]], 1)], 0
    )
    mixed = jnp.dot(mid_real, stacked, precision=lax.Precision.HIGH)
    size = mid.shape[1]
    mixed = mixed.reshape(2, size, 4, order).transpose(2, 1, 0, 3).reshape(peers, 2 * order)
    low_real = jnp.concatenate(
        [jnp.concatenate([low[0].T, low[1].T], 1), jnp.concatenate([-low[1].T, low[0].T], 1)], 0
    )
    last = jnp.dot(mixed, low_real, precision=lax.Precision.HIGH)
    back = lax.all_to_all(last.reshape(peers, 2, order), AXES, 0, 0, tiled=True)
    return jnp.transpose(back.reshape(rows, -1, 2, order), (2, 0, 1, 3))


def solution(mesh):
    return jax.shard_map(
        body,
        mesh=mesh,
        in_specs=(P(None, AXES, None, None), P(), P(), P(), P(), P()),
        out_specs=P(None, AXES, None, None),
        check_vma=False,
    )
```

time: 167 us -> 130 us (0.78)
  waiting for transfers between devices: 84.7 us -> 31.8 us
  blocking collectives: 0 us -> 43.4 us
  starting transfers between devices: 60.7 us -> 24.3 us
  other arithmetic: 6.42 us -> 20.5 us
  local copies, waits for them, and re-layouts: 10.1 us -> 5.95 us
    all_to_all x0 -> x1, blocking collectives: none -> 43.4 us  [body(): back = lax.all_to_all(last.reshape(peers, 2, order), AXES, 0, 0, tiled=True)]
    ppermute x2 -> x0, waiting for transfers between devices: 26.5 us -> none  [partner_2(): return lax.ppermute(block, axis, route)]
    all_to_all x2 -> x1, waiting for transfers between devices: 58.1 us -> 31.8 us  [body(): moved = lax.all_to_all(sent, AXES, 0, 0, tiled=True)]
    ppermute x2 -> x0, starting transfers between devices: 18.9 us -> none  [partner_2(): return lax.ppermute(block, axis, route)]
    add x1 -> x4, other arithmetic: 2.59 us -> 20.3 us  [the longest x2 10.3 us: combine(): own[0] * mine[0] - own[1] * mine[1]]
    all_to_all x2 -> x1, starting transfers between devices: 41.8 us -> 24.3 us  [body(): moved = lax.all_to_all(sent, AXES, 0, 0, tiled=True)]
    gather x12 -> x0, local copies, waits for them, and re-layouts: 5.11 us -> none  [permuted(): return gate[:, where][:, :, where]]
    another operation x6 -> x0, other arithmetic: 3.61 us -> none  [the longest x3 2.68 us: combine(): return jnp.stack([real, imag])]
  transfers between devices with their start and end apart: 4 -> 1, of which waited for: 4 -> 1; matrix products, arithmetic and copies ran while one was open for 3% -> 3% of each run, Pallas kernels for 0% -> 0%
where the time goes in v1:
time: 130 us; the launch traced here: 129 us
  blocking collectives  43.4 us (33%)
  waiting for transfers between devices  31.8 us (24%)
  starting transfers between devices  24.3 us (19%)
  other arithmetic  20.5 us (16%)
  local copies, waits for them, and re-layouts  5.95 us (5%)
  matrix products  3.31 us (3%)
    all_to_all x1, blocking collectives, body(): back = lax.all_to_all(last.reshape(peers, 2, order), AXES, 0, 0, tiled=True)  43.4 us
    all_to_all x1, waiting for transfers between devices, body(): moved = lax.all_to_all(sent, AXES, 0, 0, tiled=True)  31.8 us
    all_to_all x1, starting transfers between devices, body(): moved = lax.all_to_all(sent, AXES, 0, 0, tiled=True)  24.3 us
    add x2, other arithmetic, combine(): own[0] * mine[0] - own[1] * mine[1]  10.3 us
    add x2, other arithmetic, combine(): own[0] * mine[1] + own[1] * mine[0]  10.1 us
  transfers between devices with their start and end apart: 1, of which 1 were waited for; matrix products, arithmetic and copies ran while one was open for 3% of the time, Pallas kernels for 0%

profile of v1, /device:TPU:1, one launch (start us, length us, event | category | flops | bytes accessed | tf_op | source)
XLA Modules:
  0.0 129.5 jit_solution(2749272724436905071)
XLA Ops:
  0.0 0.0 copy-start
  0.0 2.3 %copy.77 = f32[4,128,2,128]{3,2,1,0:T(2,128)} copy(f32[4,128,2,128]{3,1,0,2:T(8,128)} %bitcast.224) | data formatting | bytes 1048576 | tf_op jit(solution)/shard_map/transpose | solution.py:59
  2.3 0.0 copy-start.2
  2.3 0.0 copy-start.1
  2.3 24.3 %all-to-all-start = ((f32[512,2,128]{2,1,0:T(2,128)}), f32[512,2,128]{2,1,0:T(2,128)S(1)}, u32[]{:S(2)}, u32[]{:S(2)}) async-start(f32[512,2,128]{2,1,0:T(2,128)} %bitcast.9), calls=%async_computation | async-start | bytes 1048576 | tf_op jit(solution)/shard_map/all_to_all | solution.py:60
  26.6 0.0 copy-done.2
  26.6 0.0 copy-start.3
  26.6 0.7 copy-done.3
  27.3 0.1 shift-left_reduce_fusion
  27.4 0.0 copy-done.1
  27.4 0.3 convolution_bitcast_fusion.1
  27.6 0.3 fusion.32
  28.0 0.3 convolution_bitcast_fusion
  28.2 0.3 fusion.36
  28.5 0.0 copy-start.4
  28.5 0.7 fusion.49
  29.2 0.0 copy-done.4
  29.2 0.1 shift-left_reduce_fusion.2
  29.3 0.2 fusion.40
  29.5 0.2 fusion.39
  29.8 0.2 convolution_subtract_fusion
  30.0 0.2 fusion.51
  30.2 0.0 copy-done
  30.2 0.3 convolution_bitcast_fusion.2
  30.5 0.3 fusion.28
  30.8 31.8 %all-to-all-done = f32[512,2,128]{2,1,0:T(2,128)S(1)} async-done(((f32[512,2,128]{2,1,0:T(2,128)}), f32[512,2,128]{2,1,0:T(2,128)S(1)}, u32[]{:S(2)}, u32[]{:S(2)}) %all-to-all-start) | async-done | bytes 524320 | tf_op jit(solution)/shard_map/all_to_all | solution.py:60
  62.6 5.1 %add_bitcast_fusion.7 = (f32[128,128]{1,0:T(8,128)S(1)}, f32[1,128,1,128]{3,1,2,0:T(8,128)S(1)}, f32[1,128,1,128]{3,1,2,0:T(8,128)S(1)}, f32[1,128,1,128]{3,1,2,0:T(8,128)S(1)}, f32[1,128,1,128]{3,1,2,0:T(8,128)S(1)}) fusion(f32[]{:T(128)} %bitcast.16, f32[]{:T(128)} %bitcast.15, f32[]{:T(128)} %bitcast.14, f32[]{:T(128)} %bitcast.5, ...), kind=kLoop, calls=%fused_computation.55 | loop fusion | flops 573440 | bytes 852000 | tf_op jit(solution)/shard_map/add | solution.py:40
  67.7 5.1 %add_bitcast_fusion.5 = (f32[128,128]{1,0:T(8,128)S(1)}, f32[1,128,1,128]{3,1,2,0:T(8,128)S(1)}, f32[1,128,1,128]{3,1,2,0:T(8,128)S(1)}, f32[1,128,1,128]{3,1,2,0:T(8,128)S(1)}, f32[1,128,1,128]{3,1,2,0:T(8,128)S(1)}) fusion(f32[]{:T(128)} %bitcast.16, f32[]{:T(128)} %bitcast.15, f32[]{:T(128)} %bitcast.14, f32[]{:T(128)} %bitcast.5, ...), kind=kLoop, calls=%fused_computation.53 | loop fusion | flops 573440 | bytes 852000 | tf_op jit(solution)/shard_map/add | solution.py:40
  72.9 5.0 %add_bitcast_fusion.6 = (f32[128,128]{1,0:T(8,128)S(1)}, f32[128,128]{1,0:T(8,128)S(1)}, f32[128,128]{1,0:T(8,128)S(1)}) fusion(f32[1,128,1,128]{3,1,2,0:T(8,128)S(1)} %get-tuple-element.7, f32[1,128,1,128]{3,1,2,0:T(8,128)S(1)} %get-tuple-element.6, f32[1,128,1,128]{3,1,2,0:T(8,128)S(1)} %get-tuple-element.9, f32[1,128,1,128]{3,1,2,0:T(8,128)S(1)} %get-tuple-element.8, ...), kind=kLoop, calls=%fused_computation.54 | loop fusion | flops 344064 | bytes 458784 | tf_op jit(solution)/shard_map/add | solution.py:41
  77.9 5.0 %add_bitcast_fusion.4 = (f32[128,128]{1,0:T(8,128)S(1)}, f32[128,128]{1,0:T(8,128)S(1)}, f32[128,128]{1,0:T(8,128)S(1)}) fusion(f32[1,128,1,128]{3,1,2,0:T(8,128)S(1)} %get-tuple-element.12, f32[1,128,1,128]{3,1,2,0:T(8,128)S(1)} %get-tuple-element.11, f32[1,128,1,128]{3,1,2,0:T(8,128)S(1)} %get-tuple-element.14, ...), kind=kLoop, calls=%fused_computation.52 | loop fusion | flops 344064 | bytes 458784 | tf_op jit(solution)/shard_map/add | solution.py:41
  83.0 0.4 fusion
  83.4 0.2 reshape.207
  83.6 0.4 copy.87
  84.0 0.4 reshape.237
  84.4 0.4 fusion.52
  84.9 0.4 copy.88
  85.3 43.4 %all_to_all.10 = f32[512,2,128]{2,1,0:T(2,128)S(1)} all-to-all(f32[512,2,128]{2,1,0:T(2,128)S(1)} %copy.88), channel_id=1, replica_groups=mesh['hi'=4,'lo'=128] {'hi','lo'}, dimensions={0} | all-to-all | bytes 1048576 | tf_op jit(solution)/shard_map/all_to_all | solution.py:76
  128.6 0.8 copy.99
  (6 shorter events, 0.1 us)
Async XLA Ops:
  0.0 30.2 %copy-start = (f32[2,128,128]{2,1,0:T(8,128)S(1)}, f32[2,128,128]{2,1,0:T(8,128)}, u32[]{:S(2)}) copy-start(f32[2,128,128]{2,1,0:T(8,128)} %param.10) | copy-start | bytes 393220
  2.3 24.3 %copy-start.2 = (f32[2,2,2,2]{3,2,1,0:T(2,128)S(1)}, f32[2,2,2,2]{3,2,1,0:T(2,128)}, u32[]{:S(2)}) copy-start(f32[2,2,2,2]{3,2,1,0:T(2,128)} %param.9) | copy-start | bytes 196
  2.3 25.1 %copy-start.1 = (f32[2,2,128,128]{3,2,1,0:T(8,128)S(1)}, f32[2,2,128,128]{3,2,1,0:T(8,128)}, u32[]{:S(2)}) copy-start(f32[2,2,128,128]{3,2,1,0:T(8,128)} %param.7) | copy-start | bytes 786436
  2.3 60.3 %all-to-all-start = ((f32[512,2,128]{2,1,0:T(2,128)}), f32[512,2,128]{2,1,0:T(2,128)S(1)}, u32[]{:S(2)}, u32[]{:S(2)}) async-start(f32[512,2,128]{2,1,0:T(2,128)} %bitcast.9), calls=%async_computation | async-start | bytes 1048576 | tf_op jit(solution)/shard_map/all_to_all | solution.py:60
  26.6 0.7 copy-start.3
  28.5 0.7 copy-start.4

commit v2 on v1

v2 whole, which is shorter than its diff:
```python
import jax
import jax.numpy as jnp
from jax import lax
from jax.experimental import pallas as pl
from jax.experimental.pallas import tpu as pltpu
from jax.sharding import PartitionSpec as P

AXES = ("hi", "lo")
HIGHEST = lax.Precision.HIGHEST
IN_VMEM = pl.BlockSpec(memory_space=pltpu.VMEM)


def index_map(order):
    count = order.shape[0]
    values = jnp.arange(2**count, dtype=jnp.int32)
    places = jnp.arange(count, dtype=jnp.int32)
    bits = values[:, None] >> places[None, :] & 1
    return jnp.sum(bits << order[None, :], axis=1)


def permuted(gate, order):
    where = index_map(order)
    pick = (where[:, None] == jnp.arange(gate.shape[-1])[None, :]).astype(gate.dtype)
    half = jnp.einsum("ai,cij->caj", pick, gate, precision=HIGHEST)
    return jnp.einsum("caj,bj->cab", half, pick, precision=HIGHEST)


def product(left, right):
    def prod(a, b):
        return jnp.dot(a, b, precision=HIGHEST)

    return jnp.stack(
        [
            prod(left[0], right[0]) - prod(left[1], right[1]),
            prod(left[0], right[1]) + prod(left[1], right[0]),
        ]
    )


def as_real(matrix):
    return jnp.concatenate(
        [
            jnp.concatenate([matrix[0], -matrix[1]], axis=1),
            jnp.concatenate([matrix[1], matrix[0]], axis=1),
        ],
        axis=0,
    )


def split(value):
    top = value.astype(jnp.bfloat16)
    return top, (value - top.astype(jnp.float32)).astype(jnp.bfloat16)


def dot3(left, right):
    def prod(a, b):
        return jnp.dot(a, b, preferred_element_type=jnp.float32)

    (left_top, left_rest), (right_top, right_rest) = split(left), split(right)
    return prod(left_top, right_rest) + prod(left_rest, right_top) + prod(left_top, right_top)


def combine(mine, other, own, cross):
    return (
        own[0] * mine[0] - own[1] * mine[1] + (cross[0] * other[0] - cross[1] * other[1]),
        own[0] * mine[1] + own[1] * mine[0] + (cross[0] * other[1] + cross[1] * other[0]),
    )


def middle_kernel(moved_ref, units_ref, mid_ref, low_ref, out_ref):
    rows, order = moved_ref.shape
    size = rows // 8

    def unit(qubit, into, source):
        at = qubit * 8 + into * 2 + source
        return units_ref[at : at + 1, :], units_ref[at + 4 : at + 5, :]

    parts = [
        tuple(moved_ref[pl.ds(h * size * 2 + c, size, 2), :] for c in range(2)) for h in range(4)
    ]
    for qubit in range(2):
        levels = [h >> qubit & 1 for h in range(4)]
        parts = [
            combine(
                parts[h],
                parts[h ^ 1 << qubit],
                unit(qubit, levels[h], levels[h]),
                unit(qubit, levels[h], 1 - levels[h]),
            )
            for h in range(4)
        ]
    stacked = jnp.concatenate([jnp.concatenate([re, im], axis=0) for re, im in parts], axis=1)
    mixed = dot3(mid_ref[...], stacked)
    turned = jnp.concatenate(
        [
            jnp.concatenate(
                [
                    mixed[c * size : (c + 1) * size, h * order : (h + 1) * order]
                    for c in range(2)
                ],
                axis=1,
            )
            for h in range(4)
        ],
        axis=0,
    )
    last = dot3(turned, low_ref[...])
    for c in range(2):
        out_ref[pl.ds(c, rows // 2, 2), :] = last[:, c * order : (c + 1) * order]


def interleave_kernel(state_ref, out_ref):
    half = state_ref.shape[1]
    for c in range(2):
        out_ref[pl.ds(c, half, 2), :] = state_ref[c]


def separate_kernel(rows_ref, out_ref):
    half = out_ref.shape[1]
    for c in range(2):
        out_ref[c] = rows_ref[pl.ds(c, half, 2), :]


def call(kernel, shape, *operands):
    return pl.pallas_call(
        kernel,
        out_shape=jax.ShapeDtypeStruct(shape, jnp.float32),
        in_specs=[IN_VMEM] * len(operands),
        out_specs=IN_VMEM,
        compiler_params=pltpu.CompilerParams(vmem_limit_bytes=32 * 2**20),
    )(*operands)


def exchange(rows, peers):
    moved = lax.all_to_all(rows.reshape(peers, 2, -1), AXES, 0, 0, tiled=True)
    return moved.reshape(rows.shape)


def body(state, low_gates, low_order, high_gates, mid_gate, mid_order):
    order = state.shape[3]
    peers = state.shape[1] * state.shape[2]
    low = product(permuted(low_gates[1], low_order[1]), permuted(low_gates[0], low_order[0]))
    mid = permuted(mid_gate, mid_order)
    units = jnp.broadcast_to(high_gates.reshape(16, 1), (16, order))
    sent = call(interleave_kernel, (2 * peers, order), state.reshape(2, peers, order))
    moved = exchange(sent, peers)
    done = call(middle_kernel, moved.shape, moved, units, as_real(mid), as_real(low).T)
    back = exchange(done, peers)
    return call(separate_kernel, (2, peers, order), back).reshape(state.shape)


def solution(mesh):
    return jax.shard_map(
        body,
        mesh=mesh,
        in_specs=(P(None, AXES, None, None), P(), P(), P(), P(), P()),
        out_specs=P(None, AXES, None, None),
        check_vma=False,
    )
```

time: 130 us -> 108 us (0.83)
  other arithmetic: 20.5 us -> 0.22 us
  local copies, waits for them, and re-layouts: 5.95 us -> 2.65 us
  Pallas kernels: 0 us -> 2.62 us
    add x4 -> x0, other arithmetic: 20.3 us -> none  [the longest x2 10.3 us: combine(): own[0] * mine[0] - own[1] * mine[1]]
    transpose x2 -> x0, local copies, waits for them, and re-layouts: 2.68 us -> none  [the longest x1 2.27 us: body(): sent = jnp.transpose(state, (1, 2, 0, 3)).reshape(peers, 2, order)]
    pallas_call x0 -> x3, Pallas kernels: none -> 2.62 us  [call(): pl.pallas_call(kernel, out_shape=jax.ShapeDtypeStruct(shape, jnp.float32)...]
    unnamed x10 -> x12, local copies, waits for them, and re-layouts: 0.68 us -> 2.48 us
    reshape x3 -> x0, local copies, waits for them, and re-layouts: 1.43 us -> none  [the longest x1 0.83 us: body(): return jnp.transpose(back.reshape(rows, -1, 2, order), (2, 0, 1, 3))]
where the time goes in v2:
time: 108 us; the launch traced here: 107 us
  blocking collectives  43.3 us (40%)
  waiting for transfers between devices  31.3 us (29%)
  starting transfers between devices  24.3 us (22%)
  matrix products  2.83 us (3%)
  local copies, waits for them, and re-layouts  2.65 us (2%)
  Pallas kernels  2.62 us (2%)
    all_to_all x1, blocking collectives, exchange(): moved = lax.all_to_all(rows.reshape(peers, 2, -1), AXES, 0, 0, tiled=True)  43.3 us
    all_to_all x1, waiting for transfers between devices, exchange(): moved = lax.all_to_all(rows.reshape(peers, 2, -1), AXES, 0, 0, tiled=True)  31.3 us
    all_to_all x1, starting transfers between devices, exchange(): moved = lax.all_to_all(rows.reshape(peers, 2, -1), AXES, 0, 0, tiled=True)  24.3 us
    pallas_call x3, Pallas kernels, call(): pl.pallas_call(kernel, out_shape=jax.ShapeDtypeStruct(shape, jnp.float32)...  2.62 us
    unnamed x12, local copies, waits for them, and re-layouts  2.48 us
  transfers between devices with their start and end apart: 1, of which 1 were waited for; matrix products, arithmetic and copies ran while one was open for 3% of the time, Pallas kernels for 0%

profile of v2, /device:TPU:1, one launch (start us, length us, event | category | flops | bytes accessed | tf_op | source)
XLA Modules:
  0.0 107.4 jit_solution(17014269799469770976)
XLA Ops:
  0.0 0.0 copy-start
  0.0 0.0 copy-start.1
  0.0 1.1 %copy-done.1 = f32[2,4,128,128]{3,2,1,0:T(8,128)S(1)} copy-done((f32[2,4,128,128]{3,2,1,0:T(8,128)S(1)}, f32[2,4,128,128]{3,2,1,0:T(8,128)}, u32[]{:S(2)}) %copy-start.1) | copy-done | bytes 524312
  1.1 0.8 shard_map.64
  1.9 0.0 copy-start.5
  1.9 24.3 %all-to-all-start = ((f32[512,2,128]{2,1,0:T(2,128)}), f32[512,2,128]{2,1,0:T(2,128)S(1)}, u32[]{:S(2)}, u32[]{:S(2)}) async-start(f32[512,2,128]{2,1,0:T(2,128)} %bitcast.1), calls=%async_computation | async-start | bytes 1048576 | tf_op jit(solution)/shard_map/all_to_all | solution.py:135
  26.2 0.0 copy-done.5
  26.2 0.1 shift-left_reduce_fusion.2
  26.3 0.0 copy-done
  26.3 0.3 convolution_bitcast_fusion.2
  26.6 0.3 fusion.5
  26.9 0.0 copy-start.4
  26.9 0.0 copy-start.3
  27.0 0.6 copy-done.4
  27.6 0.0 copy-start.2
  27.6 0.1 shift-left_reduce_fusion
  27.7 0.0 copy-done.3
  27.7 0.1 broadcast_in_dim.4
  27.8 0.7 copy-done.2
  28.6 0.3 convolution_bitcast_fusion.1
  28.8 0.3 fusion.9
  29.1 0.3 convolution_bitcast_fusion
  29.4 0.3 fusion.13
  29.7 0.3 fusion.17
  30.0 0.3 fusion.16
  30.3 0.3 convolution_subtract_fusion
  30.6 0.3 fusion.25
  30.9 31.3 %all-to-all-done = f32[512,2,128]{2,1,0:T(2,128)S(1)} async-done(((f32[512,2,128]{2,1,0:T(2,128)}), f32[512,2,128]{2,1,0:T(2,128)S(1)}, u32[]{:S(2)}, u32[]{:S(2)}) %all-to-all-start) | async-done | bytes 524320 | tf_op jit(solution)/shard_map/all_to_all | solution.py:135
  62.2 0.1 broadcast_in_dim.5.units_ref
  62.3 1.0 shard_map.65
  63.2 43.3 %all_to_all.10 = f32[512,2,128]{2,1,0:T(2,128)S(1)} all-to-all(f32[512,2,128]{2,1,0:T(2,128)S(1)} %bitcast.67), channel_id=1, replica_groups=mesh['hi'=4,'lo'=128] {'hi','lo'}, dimensions={0} | all-to-all | bytes 1048576 | tf_op jit(solution)/shard_map/all_to_all | solution.py:135
  106.6 0.8 shard_map.66
  (5 shorter events, 0.1 us)
Async XLA Ops:
  0.0 26.3 %copy-start = (f32[2,128,128]{2,1,0:T(8,128)S(1)}, f32[2,128,128]{2,1,0:T(8,128)}, u32[]{:S(2)}) copy-start(f32[2,128,128]{2,1,0:T(8,128)} %param.10) | copy-start | bytes 393220
  0.0 1.1 %copy-start.1 = (f32[2,4,128,128]{3,2,1,0:T(8,128)S(1)}, f32[2,4,128,128]{3,2,1,0:T(8,128)}, u32[]{:S(2)}) copy-start(f32[2,4,128,128]{3,2,1,0:T(8,128)} %param.6) | copy-start | bytes 1572868
  1.9 24.3 %copy-start.5 = (s32[7]{0:T(128)S(1)}, s32[7]{0:T(128)}, u32[]{:S(2)}) copy-start(s32[7]{0:T(128)} %param.11) | copy-start | bytes 88
  1.9 60.3 %all-to-all-start = ((f32[512,2,128]{2,1,0:T(2,128)}), f32[512,2,128]{2,1,0:T(2,128)S(1)}, u32[]{:S(2)}, u32[]{:S(2)}) async-start(f32[512,2,128]{2,1,0:T(2,128)} %bitcast.1), calls=%async_computation | async-start | bytes 1048576 | tf_op jit(solution)/shard_map/all_to_all | solution.py:135
  26.9 0.7 copy-start.4
  26.9 0.8 copy-start.3
  27.6 0.9 copy-start.2

commit v3 on v2

v3 whole, which is shorter than its diff:
```python
import jax
import jax.numpy as jnp
from jax import lax
from jax.experimental import pallas as pl
from jax.experimental.pallas import tpu as pltpu
from jax.sharding import Mesh
from jax.sharding import PartitionSpec as P

SIZES = {"zh": 2, "core": 2, "y": 4, "zl": 8, "x": 4}
AXES = tuple(SIZES)
GROUP = ("zh", "zl", "y", "x")
PASSES = 14
HIGHEST = lax.Precision.HIGHEST
IN_VMEM = pl.BlockSpec(memory_space=pltpu.VMEM)
IN_SMEM = pl.BlockSpec(memory_space=pltpu.SMEM)


def index_map(order):
    count = order.shape[0]
    values = jnp.arange(2**count, dtype=jnp.int32)
    places = jnp.arange(count, dtype=jnp.int32)
    bits = values[:, None] >> places[None, :] & 1
    return jnp.sum(bits << order[None, :], axis=1)


def permuted(gate, where):
    pick = (where[:, None] == jnp.arange(gate.shape[-1])[None, :]).astype(gate.dtype)
    half = jnp.einsum("ai,cij->caj", pick, gate, precision=HIGHEST)
    return jnp.einsum("caj,bj->cab", half, pick, precision=HIGHEST)


def product(left, right):
    def prod(a, b):
        return jnp.dot(a, b, precision=HIGHEST)

    return jnp.stack(
        [
            prod(left[0], right[0]) - prod(left[1], right[1]),
            prod(left[0], right[1]) + prod(left[1], right[0]),
        ]
    )


def as_real(matrix):
    return jnp.concatenate(
        [
            jnp.concatenate([matrix[0], -matrix[1]], axis=1),
            jnp.concatenate([matrix[1], matrix[0]], axis=1),
        ],
        axis=0,
    )


def split(value):
    top = value.astype(jnp.bfloat16)
    return top, (value - top.astype(jnp.float32)).astype(jnp.bfloat16)


def dot3(left, right):
    def prod(a, b):
        return jnp.dot(a, b, preferred_element_type=jnp.float32)

    (left_top, left_rest), (right_top, right_rest) = split(left), split(right)
    return prod(left_top, right_rest) + prod(left_rest, right_top) + prod(left_top, right_top)


def combine(mine, other, own, cross):
    return (
        own[0] * mine[0] - own[1] * mine[1] + (cross[0] * other[0] - cross[1] * other[1]),
        own[0] * mine[1] + own[1] * mine[0] + (cross[0] * other[1] + cross[1] * other[0]),
    )


def first_kernel(passes_ref, unit_ref, mine_ref, other_ref, out_ref):
    half = mine_ref.shape[1]
    own = (unit_ref[0:1, :], unit_ref[1:2, :])
    cross = (unit_ref[2:3, :], unit_ref[3:4, :])

    def one_pass(_, carry):
        parts = combine(
            (mine_ref[0], mine_ref[1]), (other_ref[0], other_ref[1]), own, cross
        )
        for c in range(2):
            out_ref[pl.ds(c, half, 2), :] = parts[c]
        return carry

    lax.fori_loop(0, passes_ref[0], one_pass, 0)


def middle_kernel(moved_ref, unit_ref, mid_ref, low_ref, out_ref):
    rows, order = moved_ref.shape
    size = mid_ref.shape[0] // 2

    def place(level, pair, c):
        return pl.ds(level * size * 4 + pair * 2 + c, size, 4)

    columns = []
    for pair in range(2):
        parts = [
            tuple(moved_ref[place(level, pair, c), :] for c in range(2)) for level in range(2)
        ]
        for level in range(2):
            row = level * 4
            own = (unit_ref[row : row + 1, :], unit_ref[row + 1 : row + 2, :])
            cross = (unit_ref[row + 2 : row + 3, :], unit_ref[row + 3 : row + 4, :])
            columns.append(
                jnp.concatenate(combine(parts[level], parts[1 - level], own, cross), axis=0)
            )
    mixed = dot3(mid_ref[...], jnp.concatenate(columns, axis=1))
    turned = jnp.concatenate(
        [
            jnp.concatenate(
                [
                    mixed[c * size : (c + 1) * size, at * order : (at + 1) * order]
                    for c in range(2)
                ],
                axis=1,
            )
            for at in range(4)
        ],
        axis=0,
    )
    last = dot3(turned, low_ref[...])
    for pair in range(2):
        for level in range(2):
            at = (pair * 2 + level) * size
            for c in range(2):
                out_ref[place(level, pair, c), :] = last[
                    at : at + size, c * order : (c + 1) * order
                ]


def last_kernel(rows_ref, out_ref):
    half = out_ref.shape[1]
    for c in range(2):
        out_ref[c] = rows_ref[pl.ds(c, half, 2), :]


def call(kernel, shape, *operands, specs=None):
    return pl.pallas_call(
        kernel,
        out_shape=jax.ShapeDtypeStruct(shape, jnp.float32),
        in_specs=specs or [IN_VMEM] * len(operands),
        out_specs=IN_VMEM,
        compiler_params=pltpu.CompilerParams(vmem_limit_bytes=32 * 2**20),
    )(*operands)


def exchange(rows):
    moved = lax.all_to_all(rows.reshape(256, 4, -1), GROUP, 0, 0, tiled=True)
    return moved.reshape(rows.shape)


def level_units(unit, order):
    rows = jnp.stack(
        [unit[c, level, level ^ flip] for level in range(2) for flip in range(2) for c in range(2)]
    )
    return jnp.broadcast_to(rows[:, None], (8, order))


def body(state, low_gates, low_order, high_gates, mid_gate, mid_order):
    order = state.shape[3]
    pairs = state.shape[1] * state.shape[2]
    core = lax.axis_index("core")

    mine = state.reshape(2, pairs, order)
    other = lax.ppermute(mine, "core", [(0, 1), (1, 0)])
    both = level_units(high_gates[0], order)
    unit = jnp.where(core == 0, both, jnp.roll(both, 4, axis=0))
    passes = jnp.where(core == 0, 1, PASSES).astype(jnp.int32).reshape(1)
    sent = call(
        first_kernel,
        (2 * pairs, order),
        passes,
        unit,
        mine,
        other,
        specs=[IN_SMEM] + [IN_VMEM] * 3,
    )
    moved = exchange(sent)

    low = product(
        permuted(low_gates[1], index_map(low_order[1])),
        permuted(low_gates[0], index_map(low_order[0])),
    )
    where = index_map(mid_order).reshape(4, 8, 4).transpose(1, 0, 2).reshape(-1)
    mid = permuted(mid_gate, where)
    done = call(
        middle_kernel,
        moved.shape,
        moved,
        level_units(high_gates[1], order),
        as_real(mid),
        as_real(low).T,
    )
    back = exchange(done)
    return call(last_kernel, (2, pairs, order), back).reshape(state.shape)


def solution(mesh):
    mesh = Mesh(mesh.devices.reshape(tuple(SIZES.values())), AXES)
    return jax.shard_map(
        body,
        mesh=mesh,
        in_specs=(P(None, AXES, None, None), P(), P(), P(), P(), P()),
        out_specs=P(None, AXES, None, None),
        check_vma=False,
    )
```

time: 108 us -> 121 us (1.12)
  the two profiles are of different devices: /device:TPU:1 before, /device:TPU:2 now
where the time goes in v3:
time: 121 us
  blocking collectives  44.6 us (37%)
  waiting for transfers between devices  27.3 us (23%)
  starting transfers between devices  25.7 us (21%)
  local copies, waits for them, and re-layouts  11.3 us (9%)
  other arithmetic  5.31 us (4%)
  matrix products  3.81 us (3%)
  Pallas kernels  2.59 us (2%)
    all_to_all x1, blocking collectives, exchange(): moved = lax.all_to_all(rows.reshape(256, 4, -1), GROUP, 0, 0, tiled=True)  44.6 us
    all_to_all x1, waiting for transfers between devices, exchange(): moved = lax.all_to_all(rows.reshape(256, 4, -1), GROUP, 0, 0, tiled=True)  27.3 us
    all_to_all x1, starting transfers between devices, exchange(): moved = lax.all_to_all(rows.reshape(256, 4, -1), GROUP, 0, 0, tiled=True)  23.7 us
    another operation x2, local copies, waits for them, and re-layouts, level_units(): jnp.stack([unit[c, level, level ^ flip] for level in range(2) for flip in...  10.2 us
    select_n x1, other arithmetic, body(): unit = jnp.where(core == 0, both, jnp.roll(both, 4, axis=0))  5.09 us
    pallas_call x3, Pallas kernels, call(): pl.pallas_call(kernel, out_shape=jax.ShapeDtypeStruct(shape, jnp.float32)...  2.59 us
  transfers between devices with their start and end apart: 2, of which 1 were waited for; matrix products, arithmetic and copies ran while one was open for 17% of the time, Pallas kernels for 0%

profile of v3, /device:TPU:2, one launch (start us, length us, event | category | flops | bytes accessed | tf_op | source)
XLA Modules:
  0.0 120.9 jit_solution(4296108001169500986)
XLA Ops:
  0.0 0.0 copy-start
  0.0 0.0 copy-start.4
  0.0 2.0 %collective-permute-start = (f32[2,512,128]{2,1,0:T(8,128)}, f32[2,512,128]{2,1,0:T(8,128)S(1)}, u32[]{:S(2)}, u32[]{:S(2)}) collective-permute-start(f32[2,512,128]{2,1,0:T(8,128)} %bitcast.91), channel_id=1, source_target_pairs={{0,128},{128,0},{1,129},{129,1},{2,130},{130,2},{3,131},{131,3},{4... | collective-permute-start | bytes 1572872 | tf_op jit(solution)/shard_map/ppermute | solution.py:167
  2.1 0.0 copy-done.4
  2.1 0.0 copy-start.3
  2.1 0.1 shift-left_reduce_fusion
  2.2 0.0 copy-start.2
  2.2 0.0 copy-start.1
  2.2 1.2 %convolution_bitcast_fusion = f32[2,128,128]{2,1,0:T(8,128)S(1)} fusion(f32[2,2,128,128]{3,2,1,0:T(8,128)} %param.7, s32[128]{0:T(128)S(1)} %get-tuple-element.37), kind=kOutput, calls=%fused_computation | convolution fusion | flops 50348032 | bytes 262656 | tf_op jit(solution)/shard_map/ai,cij->caj/dot_general | solution.py:28
  3.4 0.3 fusion.13
  3.7 0.0 copy-done.3
  3.8 0.7 fusion.26
  4.5 5.1 %stack.10 = f32[8]{0:T(128)S(1)} concatenate(f32[1]{0:T(128)} %bitcast.2, f32[1]{0:T(128)} %bitcast.3, f32[1]{0:T(128)} %bitcast.4, f32[1]{0:T(128)} %bitcast.5, f32[1]{0:T(128)} %bitcast.6, f32[1]{0:T(128)} %bitcast.7, f32[1]{0:T(128)} %bitcast.8, f32[1]{0:T(128)} %bitcast.9), dimensions={0} | concatenate | bytes 64 | tf_op jit(solution)/shard_map/stack | solution.py:155
  9.6 5.1 %broadcast_select_fusion = f32[8]{0:T(128)S(1)} fusion(f32[8]{0:T(128)S(1)} %stack.10, pred[]{:T(512)S(6)} %eq.22, f32[1]{0:T(128)} %bitcast.5, f32[1]{0:T(128)} %bitcast.4, f32[1]{0:T(128)} %bitcast.3, f32[1]{0:T(128)} %bitcast.2, f32[1]{0:T(128)} %bitcast.9, f32[1]{0:T(128)} %bitcast.8, f32[1]{0:T(128)} %bitcast.7, f32[1]{0:T(128)} %bitcast.6), kind=kLoop, calls=%fused_computation.40 | loop fusion | flops 64 | bytes 97 | tf_op jit(solution)/shard_map/jit(_where)/select_n | solution.py:169
  14.7 0.0 copy-done.2
  14.7 0.3 convolution_bitcast_fusion.1
  14.9 0.3 fusion.9
  15.2 0.0 collective-permute-done.other_ref
  15.2 0.1 broadcast.15.unit_ref
  15.3 0.0 copy-done.1
  15.3 0.9 shard_map.64
  16.2 0.0 copy-start.5
  16.2 23.7 %all-to-all-start = ((f32[256,4,128]{2,1,0:T(4,128)}), f32[256,4,128]{2,1,0:T(4,128)S(1)}, u32[]{:S(2)}, u32[]{:S(2)}) async-start(f32[256,4,128]{2,1,0:T(4,128)} %bitcast.11), calls=%async_computation | async-start | bytes 1048576 | tf_op jit(solution)/shard_map/all_to_all | solution.py:150
  39.9 0.0 copy-done.5
  39.9 0.1 shift-left_reduce_fusion.2
  40.0 0.1 reshape.34
  40.2 0.1 eq.46
  40.3 5.1 %stack.13 = f32[8]{0:T(128)S(1)} concatenate(f32[1]{0:T(128)} %bitcast.14, f32[1]{0:T(128)} %bitcast.15, f32[1]{0:T(128)} %bitcast.16, f32[1]{0:T(128)} %bitcast.17, f32[1]{0:T(128)} %bitcast.18, f32[1]{0:T(128)} %bitcast.19, f32[1]{0:T(128)} %bitcast.20, f32[1]{0:T(128)} %bitcast.21), dimensions={0} | concatenate | bytes 64 | tf_op jit(solution)/shard_map/stack | solution.py:155
  45.3 0.3 fusion.16
  45.6 0.3 fusion.17
  45.9 0.3 convolution_subtract_fusion
  46.2 0.3 fusion.28
  46.6 0.0 copy-done
  46.6 0.3 convolution_bitcast_fusion.2
  46.8 0.3 fusion.5
  47.2 27.3 %all-to-all-done = f32[256,4,128]{2,1,0:T(4,128)S(1)} async-done(((f32[256,4,128]{2,1,0:T(4,128)}), f32[256,4,128]{2,1,0:T(4,128)S(1)}, u32[]{:S(2)}, u32[]{:S(2)}) %all-to-all-start) | async-done | bytes 524320 | tf_op jit(solution)/shard_map/all_to_all | solution.py:150
  74.6 0.1 broadcast_in_dim.11.unit_ref
  74.6 0.8 shard_map.65
  75.5 44.6 %all_to_all.10 = f32[256,4,128]{2,1,0:T(4,128)S(1)} all-to-all(f32[256,4,128]{2,1,0:T(4,128)S(1)} %bitcast.89), channel_id=1, replica_groups=mesh['zh'=2,'core'=2,'y'=4,'zl'=8,'x'=4] {'zh','zl','y','x'}, dimensions={0} | all-to-all | bytes 1048576 | tf_op jit(solution)/shard_map/all_to_all | solution.py:150
  120.1 0.8 shard_map.66
  (7 shorter events, 0.1 us)
Async XLA Ops:
  0.0 46.6 %copy-start = (f32[2,128,128]{2,1,0:T(8,128)S(1)}, f32[2,128,128]{2,1,0:T(8,128)}, u32[]{:S(2)}) copy-start(f32[2,128,128]{2,1,0:T(8,128)} %param.10) | copy-start | bytes 393220
  0.0 2.1 %copy-start.4 = (s32[2,7]{1,0:T(2,128)S(1)}, s32[2,7]{1,0:T(2,128)}, u32[]{:S(2)}) copy-start(s32[2,7]{1,0:T(2,128)} %param.8) | copy-start | bytes 172
  0.0 15.2 %collective-permute-start = (f32[2,512,128]{2,1,0:T(8,128)}, f32[2,512,128]{2,1,0:T(8,128)S(1)}, u32[]{:S(2)}, u32[]{:S(2)}) collective-permute-start(f32[2,512,128]{2,1,0:T(8,128)} %bitcast.91), channel_id=1, source_target_pairs={{0,128},{128,0},{1,129},{129,1},{2,130},{130,2},{3,131},{131,3},{4... | collective-permute-start | bytes 1572872 | tf_op jit(solution)/shard_map/ppermute | solution.py:167
  2.1 1.7 %copy-start.3 = (f32[2,2,2,2]{3,2,1,0:T(2,128)S(1)}, f32[2,2,2,2]{3,2,1,0:T(2,128)}, u32[]{:S(2)}) copy-start(f32[2,2,2,2]{3,2,1,0:T(2,128)} %param.9) | copy-start | bytes 196
  2.2 12.5 %copy-start.2 = (f32[2,2,128,128]{3,2,1,0:T(8,128)S(1)}, f32[2,2,128,128]{3,2,1,0:T(8,128)}, u32[]{:S(2)}) copy-start(f32[2,2,128,128]{3,2,1,0:T(8,128)} %param.7) | copy-start | bytes 786436
  2.2 13.1 %copy-start.1 = (f32[2,4,128,128]{3,2,1,0:T(8,128)S(1)}, f32[2,4,128,128]{3,2,1,0:T(8,128)}, u32[]{:S(2)}) copy-start(f32[2,4,128,128]{3,2,1,0:T(8,128)} %param.6) | copy-start | bytes 1572868
  16.2 23.7 %copy-start.5 = (s32[7]{0:T(128)S(1)}, s32[7]{0:T(128)}, u32[]{:S(2)}) copy-start(s32[7]{0:T(128)} %param.11) | copy-start | bytes 88
  16.2 58.3 %all-to-all-start = ((f32[256,4,128]{2,1,0:T(4,128)}), f32[256,4,128]{2,1,0:T(4,128)S(1)}, u32[]{:S(2)}, u32[]{:S(2)}) async-start(f32[256,4,128]{2,1,0:T(4,128)} %bitcast.11), calls=%async_computation | async-start | bytes 1048576 | tf_op jit(solution)/shard_map/all_to_all | solution.py:150

commit v4 on v3

v4 whole, which is shorter than its diff:
```python
import jax
import jax.numpy as jnp
from jax import lax
from jax.experimental import pallas as pl
from jax.experimental.pallas import tpu as pltpu
from jax.sharding import Mesh
from jax.sharding import PartitionSpec as P

SIZES = {"zh": 2, "core": 2, "y": 4, "zl": 8, "x": 4}
AXES = tuple(SIZES)
GROUP = ("zh", "zl", "y", "x")
PASSES = 90
LATE = 0
HIGHEST = lax.Precision.HIGHEST
IN_VMEM = pl.BlockSpec(memory_space=pltpu.VMEM)
IN_SMEM = pl.BlockSpec(memory_space=pltpu.SMEM)


def split(value):
    top = value.astype(jnp.bfloat16)
    return top, (value - top.astype(jnp.float32)).astype(jnp.bfloat16)


def dot3(left, right):
    def prod(a, b):
        return jnp.dot(a, b, preferred_element_type=jnp.float32)

    (left_top, left_rest), (right_top, right_rest) = split(left), split(right)
    return prod(left_top, right_rest) + prod(left_rest, right_top) + prod(left_top, right_top)


def combine(mine, other, own, cross):
    return (
        own[0] * mine[0] - own[1] * mine[1] + (cross[0] * other[0] - cross[1] * other[1]),
        own[0] * mine[1] + own[1] * mine[0] + (cross[0] * other[1] + cross[1] * other[0]),
    )


def pick_rows(order_ref, at, number):
    count = order_ref.shape[1]
    where = jnp.zeros_like(number)
    for j in range(count):
        where += (number >> j & 1) << order_ref[at, j]
    return (where == lax.broadcasted_iota(jnp.int32, number.shape, 1)).astype(jnp.float32)


def gates_kernel(low_order_ref, mid_order_ref, low_gates_ref, mid_gate_ref, mid_ref, low_ref):
    size = mid_gate_ref.shape[1]
    number = lax.broadcasted_iota(jnp.int32, (size, size), 0)
    group = (number >> 2 & 3) << 5 | (number >> 4 & 7) << 2 | number & 3

    def dot(left, right):
        return jnp.dot(left, right, precision=HIGHEST, preferred_element_type=jnp.float32)

    def permuted(gate, pick):
        half = dot(pick, gate)
        return lax.dot_general(
            half,
            pick,
            (((1,), (1,)), ((), ())),
            precision=HIGHEST,
            preferred_element_type=jnp.float32,
        )

    pick = pick_rows(mid_order_ref, 0, group)
    real, imag = (permuted(mid_gate_ref[c], pick) for c in range(2))
    mid_ref[:size, :size] = real
    mid_ref[:size, size:] = -imag
    mid_ref[size:, :size] = imag
    mid_ref[size:, size:] = real
    lows = []
    for k in range(2):
        pick = pick_rows(low_order_ref, k, number)
        lows.append([permuted(low_gates_ref[k, c], pick) for c in range(2)])
    (right_re, right_im), (left_re, left_im) = lows
    real = (dot(left_re, right_re) - dot(left_im, right_im)).T
    imag = (dot(left_re, right_im) + dot(left_im, right_re)).T
    low_ref[:size, :size] = real
    low_ref[:size, size:] = imag
    low_ref[size:, :size] = -imag
    low_ref[size:, size:] = real


def core_factor(unit_ref, other):
    core = lax.axis_index("core")
    source = 1 - core if other else core
    return tuple(unit_ref[pl.ds(c * 4 + core * 2 + source, 1), :] for c in range(2))


def own_kernel(unit_ref, mine_ref, out_ref):
    re, im = core_factor(unit_ref, False)
    half = mine_ref.shape[1]
    out_ref[pl.ds(0, half, 2), :] = re * mine_ref[0] - im * mine_ref[1]
    out_ref[pl.ds(1, half, 2), :] = re * mine_ref[1] + im * mine_ref[0]


def first_kernel(unit_ref, own_ref, other_ref, out_ref):
    re, im = core_factor(unit_ref, True)
    half = other_ref.shape[1]

    def one_pass(_, carry):
        for c, add in (
            (0, re * other_ref[0] - im * other_ref[1]),
            (1, re * other_ref[1] + im * other_ref[0]),
        ):
            out_ref[pl.ds(c, half, 2), :] = own_ref[pl.ds(c, half, 2), :] + add
        return carry

    late = (lax.axis_index("core") == LATE).astype(jnp.int32)
    lax.fori_loop(0, 1 + late * PASSES, one_pass, 0)


def middle_kernel(moved_ref, unit_ref, mid_ref, low_ref, out_ref):
    rows, order = moved_ref.shape
    size = mid_ref.shape[0] // 2

    def place(level, pair, c):
        return pl.ds(level * size * 4 + pair * 2 + c, size, 4)

    def factor(into, source):
        rows = [8 + c * 4 + into * 2 + source for c in range(2)]
        return tuple(unit_ref[row : row + 1, :] for row in rows)

    columns = []
    for pair in range(2):
        parts = [
            tuple(moved_ref[place(level, pair, c), :] for c in range(2)) for level in range(2)
        ]
        for level in range(2):
            own, cross = factor(level, level), factor(level, 1 - level)
            columns.append(
                jnp.concatenate(combine(parts[level], parts[1 - level], own, cross), axis=0)
            )
    mixed = dot3(mid_ref[...], jnp.concatenate(columns, axis=1))
    turned = jnp.concatenate(
        [
            jnp.concatenate(
                [
                    mixed[c * size : (c + 1) * size, at * order : (at + 1) * order]
                    for c in range(2)
                ],
                axis=1,
            )
            for at in range(4)
        ],
        axis=0,
    )
    last = dot3(turned, low_ref[...])
    for pair in range(2):
        for level in range(2):
            at = (pair * 2 + level) * size
            for c in range(2):
                out_ref[place(level, pair, c), :] = last[
                    at : at + size, c * order : (c + 1) * order
                ]


def last_kernel(rows_ref, out_ref):
    half = out_ref.shape[1]
    for c in range(2):
        out_ref[c] = rows_ref[pl.ds(c, half, 2), :]


def call(kernel, shapes, *operands, specs=None):
    out = jax.tree.map(
        lambda shape: jax.ShapeDtypeStruct(shape, jnp.float32),
        shapes,
        is_leaf=lambda shape: isinstance(shape, tuple),
    )
    return pl.pallas_call(
        kernel,
        out_shape=out,
        in_specs=specs or [IN_VMEM] * len(operands),
        out_specs=jax.tree.map(lambda _: IN_VMEM, out),
        compiler_params=pltpu.CompilerParams(vmem_limit_bytes=32 * 2**20),
    )(*operands)


def exchange(rows):
    moved = lax.all_to_all(rows.reshape(256, 4, -1), GROUP, 0, 0, tiled=True)
    return moved.reshape(rows.shape)


def body(state, low_gates, low_order, high_gates, mid_gate, mid_order):
    order = state.shape[3]
    pairs = state.shape[1] * state.shape[2]
    rows = (2 * pairs, order)

    mine = state.reshape(2, pairs, order)
    other = lax.ppermute(mine, "core", [(0, 1), (1, 0)])
    units = jnp.broadcast_to(high_gates.reshape(16, 1), (16, order))
    own = call(own_kernel, rows, units, mine)
    sent = call(first_kernel, rows, units, own, other)
    sent, low_gates, low_order, mid_gate, mid_order = lax.optimization_barrier(
        (sent, low_gates, low_order, mid_gate, mid_order)
    )
    moved = exchange(sent)
    mid, low = call(
        gates_kernel,
        [(2 * order, 2 * order)] * 2,
        low_order,
        mid_order.reshape(1, -1),
        low_gates,
        mid_gate,
        specs=[IN_SMEM] * 2 + [IN_VMEM] * 2,
    )
    done = call(middle_kernel, rows, moved, units, mid, low)
    back = exchange(done)
    return call(last_kernel, (2, pairs, order), back).reshape(state.shape)


def solution(mesh):
    mesh = Mesh(mesh.devices.reshape(tuple(SIZES.values())), AXES)
    return jax.shard_map(
        body,
        mesh=mesh,
        in_specs=(P(None, AXES, None, None), P(), P(), P(), P(), P()),
        out_specs=P(None, AXES, None, None),
        check_vma=False,
    )
```

time: 121 us -> 99.3 us (0.82)
  Pallas kernels: 2.59 us -> 15.2 us
  blocking collectives: 44.6 us -> 33.2 us
  local copies, waits for them, and re-layouts: 11.3 us -> 2.55 us
  other arithmetic: 5.31 us -> 0 us
  waiting for transfers between devices: 27.3 us -> 22.2 us
  matrix products: 3.81 us -> 0 us
    pallas_call x3 -> x5, Pallas kernels: 2.59 us -> 15.2 us  [call(): pl.pallas_call(kernel, out_shape=out, in_specs=specs or [IN_VMEM] * len(o...]
    all_to_all x1, blocking collectives: 44.6 us -> 33.2 us  [exchange(): moved = lax.all_to_all(rows.reshape(256, 4, -1), GROUP, 0, 0, tiled=True)]
    another operation x2 -> x0, local copies, waits for them, and re-layouts: 10.2 us -> none  [level_units(): jnp.stack([unit[c, level, level ^ flip] for level in range(2) for flip in...]
    all_to_all x1, waiting for transfers between devices: 27.3 us -> 22.1 us  [exchange(): moved = lax.all_to_all(rows.reshape(256, 4, -1), GROUP, 0, 0, tiled=True)]
    select_n x1 -> x0, other arithmetic: 5.09 us -> none  [body(): unit = jnp.where(core == 0, both, jnp.roll(both, 4, axis=0))]
    dot_general x10 -> x0, matrix products: 3.81 us -> none  [the longest x3 1.74 us: permuted(): half = jnp.einsum('ai,cij->caj', pick, gate, precision=HIGHEST)]
    unnamed x12 -> x10, local copies, waits for them, and re-layouts: 0.03 us -> 1.7 us
  transfers between devices with their start and end apart: 2 -> 2, of which waited for: 1 -> 2; matrix products, arithmetic and copies ran while one was open for 17% -> 1% of each run, Pallas kernels for 0% -> 3%
where the time goes in v4:
time: 99.3 us; the launch traced here: 98.9 us
  blocking collectives  33.2 us (33%)
  starting transfers between devices  25.6 us (26%)
  waiting for transfers between devices  22.2 us (22%)
  Pallas kernels  15.2 us (15%)
  local copies, waits for them, and re-layouts  2.55 us (3%)
    all_to_all x1, blocking collectives, exchange(): moved = lax.all_to_all(rows.reshape(256, 4, -1), GROUP, 0, 0, tiled=True)  33.2 us
    all_to_all x1, starting transfers between devices, exchange(): moved = lax.all_to_all(rows.reshape(256, 4, -1), GROUP, 0, 0, tiled=True)  23.7 us
    all_to_all x1, waiting for transfers between devices, exchange(): moved = lax.all_to_all(rows.reshape(256, 4, -1), GROUP, 0, 0, tiled=True)  22.1 us
    pallas_call x5, Pallas kernels, call(): pl.pallas_call(kernel, out_shape=out, in_specs=specs or [IN_VMEM] * len(o...  15.2 us
  transfers between devices with their start and end apart: 2, of which 2 were waited for; matrix products, arithmetic and copies ran while one was open for 1% of the time, Pallas kernels for 3%

profile of v4, /device:TPU:2, one launch (start us, length us, event | category | flops | bytes accessed | tf_op | source)
XLA Modules:
  0.0 98.9 jit_solution(17912771693184170169)
XLA Ops:
  0.0 1.9 %collective-permute-start = (f32[2,512,128]{2,1,0:T(8,128)}, f32[2,512,128]{2,1,0:T(8,128)S(1)}, u32[]{:S(2)}, u32[]{:S(2)}) collective-permute-start(f32[2,512,128]{2,1,0:T(8,128)} %bitcast.10), channel_id=1, source_target_pairs={{0,128},{128,0},{1,129},{129,1},{2,130},{130,2},{3,131},{131,3},{4... | collective-permute-start | bytes 1572872 | tf_op jit(solution)/shard_map/ppermute | solution.py:190
  1.9 0.8 broadcast_in_dim.7
  2.7 0.1 broadcast_in_dim.8.unit_ref
  2.8 0.0 copy-start
  2.8 1.0 %copy-done = f32[2,4,128,128]{3,2,1,0:T(8,128)S(1)} copy-done((f32[2,4,128,128]{3,2,1,0:T(8,128)S(1)}, f32[2,4,128,128]{3,2,1,0:T(8,128)}, u32[]{:S(2)}) %copy-start) | copy-done | bytes 524312
  3.8 0.1 shard_map.64.own_ref
  3.9 0.1 collective-permute-done.other_ref
  4.0 11.0 %shard_map.65 = f32[1024,128]{1,0:T(8,128)} custom-call(f32[16,128]{1,0:T(8,128)S(1)} %broadcast_in_dim.8.unit_ref, f32[1024,128]{1,0:T(8,128)S(1)} %shard_map.64.own_ref, f32[2,512,128]{2,1,0:T(8,128)S(1)} %collective-permute-done.other_ref), custom_call_target="tpu_custom_call" | custom-call | tf_op jit(solution)/shard_map/pallas_call | solution.py:170
  15.0 0.0 copy-start.1
  15.0 0.0 copy-start.2
  15.0 23.7 %all-to-all-start = ((f32[256,4,128]{2,1,0:T(4,128)}), f32[256,4,128]{2,1,0:T(4,128)S(1)}, u32[]{:S(2)}, u32[]{:S(2)}) async-start(f32[256,4,128]{2,1,0:T(4,128)} %bitcast.1), calls=%async_computation | async-start | bytes 1048576 | tf_op jit(solution)/shard_map/all_to_all | solution.py:180
  38.7 0.0 copy-start.3
  38.7 0.0 copy-start.4
  38.7 0.0 copy-done.1
  38.7 0.0 copy-done.2
  38.7 0.6 copy-done.3
  39.3 0.0 copy-done.4
  39.3 2.5 %shard_map.66 = (f32[256,256]{1,0:T(8,128)S(1)}, f32[256,256]{1,0:T(8,128)S(1)}) custom-call(s32[2,7]{1,0:T(2,128)S(1)} %copy-done.3, s32[1,7]{1,0:T(1,128)S(1)} %bitcast.12, f32[2,2,128,128]{3,2,1,0:T(8,128)S(1)} %copy-done.1, f32[2,128,128]{2,1,0:T(8,128)S(1)} %copy-done.2), custom_call_target="tpu_custom_call" | custom-call | tf_op jit(solution)/shard_map/pallas_call | solution.py:170
  41.9 22.1 %all-to-all-done = f32[256,4,128]{2,1,0:T(4,128)S(1)} async-done(((f32[256,4,128]{2,1,0:T(4,128)}), f32[256,4,128]{2,1,0:T(4,128)S(1)}, u32[]{:S(2)}, u32[]{:S(2)}) %all-to-all-start) | async-done | bytes 524320 | tf_op jit(solution)/shard_map/all_to_all | solution.py:180
  64.0 0.8 shard_map.67
  64.8 33.2 %all_to_all.10 = f32[256,4,128]{2,1,0:T(4,128)S(1)} all-to-all(f32[256,4,128]{2,1,0:T(4,128)S(1)} %bitcast.8), channel_id=1, replica_groups=mesh['zh'=2,'core'=2,'y'=4,'zl'=8,'x'=4] {'zh','zl','y','x'}, dimensions={0} | all-to-all | bytes 1048576 | tf_op jit(solution)/shard_map/all_to_all | solution.py:180
  98.1 0.8 shard_map.68
Async XLA Ops:
  0.0 4.0 %collective-permute-start = (f32[2,512,128]{2,1,0:T(8,128)}, f32[2,512,128]{2,1,0:T(8,128)S(1)}, u32[]{:S(2)}, u32[]{:S(2)}) collective-permute-start(f32[2,512,128]{2,1,0:T(8,128)} %bitcast.10), channel_id=1, source_target_pairs={{0,128},{128,0},{1,129},{129,1},{2,130},{130,2},{3,131},{131,3},{4... | collective-permute-start | bytes 1572872 | tf_op jit(solution)/shard_map/ppermute | solution.py:190
  2.8 1.0 %copy-start = (f32[2,4,128,128]{3,2,1,0:T(8,128)S(1)}, f32[2,4,128,128]{3,2,1,0:T(8,128)}, u32[]{:S(2)}) copy-start(f32[2,4,128,128]{3,2,1,0:T(8,128)} %param.6) | copy-start | bytes 1572868
  15.0 23.7 %copy-start.1 = (f32[2,2,128,128]{3,2,1,0:T(8,128)S(1)}, f32[2,2,128,128]{3,2,1,0:T(8,128)}, u32[]{:S(2)}) copy-start(f32[2,2,128,128]{3,2,1,0:T(8,128)} %low_gates_ref) | copy-start | bytes 786436
  15.0 23.7 %copy-start.2 = (f32[2,128,128]{2,1,0:T(8,128)S(1)}, f32[2,128,128]{2,1,0:T(8,128)}, u32[]{:S(2)}) copy-start(f32[2,128,128]{2,1,0:T(8,128)} %mid_gate_ref) | copy-start | bytes 393220
  15.0 49.0 %all-to-all-start = ((f32[256,4,128]{2,1,0:T(4,128)}), f32[256,4,128]{2,1,0:T(4,128)S(1)}, u32[]{:S(2)}, u32[]{:S(2)}) async-start(f32[256,4,128]{2,1,0:T(4,128)} %bitcast.1), calls=%async_computation | async-start | bytes 1048576 | tf_op jit(solution)/shard_map/all_to_all | solution.py:180
  38.7 0.7 copy-start.3
  38.7 0.7 copy-start.4

commit v5 on v4

v5 whole, which is shorter than its diff:
```python
import jax
import jax.numpy as jnp
import numpy as np
from jax import lax
from jax.experimental import pallas as pl
from jax.experimental.pallas import tpu as pltpu
from jax.sharding import Mesh
from jax.sharding import PartitionSpec as P

AXIS = "device"
NUMBERS = np.arange(512).reshape(2, 2, 4, 8, 4).transpose(1, 0, 3, 2, 4).reshape(2, 16, 16)
LINES = [[group.tolist() for group in NUMBERS[core].T] for core in range(2)]
PLANES = [[group.tolist() for group in NUMBERS[core]] for core in range(2)]
STAGES = (LINES[0] + PLANES[1], PLANES[0] + LINES[1])
HIGHEST = lax.Precision.HIGHEST
IN_VMEM = pl.BlockSpec(memory_space=pltpu.VMEM)
IN_SMEM = pl.BlockSpec(memory_space=pltpu.SMEM)


def split(value):
    top = value.astype(jnp.bfloat16)
    return top, (value - top.astype(jnp.float32)).astype(jnp.bfloat16)


def dot3(left, right):
    def prod(a, b):
        return jnp.dot(a, b, preferred_element_type=jnp.float32)

    (left_top, left_rest), (right_top, right_rest) = split(left), split(right)
    return prod(left_top, right_rest) + prod(left_rest, right_top) + prod(left_top, right_top)


def core_of():
    return lax.axis_index(AXIS) >> 7 & 1


def pick_rows(order_ref, at, number, columns):
    where = jnp.zeros_like(number)
    for j in range(order_ref.shape[1]):
        where += (number >> j & 1) << order_ref[at, j]
    return (where == lax.broadcasted_iota(jnp.int32, columns, 1)).astype(jnp.float32)


def gates_kernel(
    low_order_ref, mid_order_ref, unit_ref, low_gates_ref, mid_gate_ref, mid_ref, low_ref
):
    size = mid_gate_ref.shape[1]
    group = 2 * size
    lines = core_of() == 0

    def parts(number):
        plane = jnp.where(lines, number >> 4, number & 15)
        line = jnp.where(lines, number & 15, number >> 4)
        return line >> 3, (plane >> 2) << 5 | (line & 7) << 2 | plane & 3

    def dot(left, right):
        return jnp.dot(left, right, precision=HIGHEST, preferred_element_type=jnp.float32)

    def permuted(gate, pick):
        return lax.dot_general(
            dot(pick, gate),
            pick,
            (((1,), (1,)), ((), ())),
            precision=HIGHEST,
            preferred_element_type=jnp.float32,
        )

    into, index = parts(lax.broadcasted_iota(jnp.int32, (group, size), 0))
    pick = pick_rows(mid_order_ref, 0, index, (group, size))
    mid_re, mid_im = (permuted(mid_gate_ref[c], pick) for c in range(2))
    into, _ = parts(lax.broadcasted_iota(jnp.int32, (group, group), 0))
    source, _ = parts(lax.broadcasted_iota(jnp.int32, (group, group), 1))

    def factor(c):
        rows = [
            jnp.concatenate([unit_ref[row : row + 1, :]] * 2, axis=1)
            for row in range(8 + c * 4, 12 + c * 4)
        ]
        return jnp.where(
            into == 0,
            jnp.where(source == 0, rows[0], rows[1]),
            jnp.where(source == 0, rows[2], rows[3]),
        )

    unit_re, unit_im = factor(0), factor(1)
    real = unit_re * mid_re - unit_im * mid_im
    imag = unit_re * mid_im + unit_im * mid_re
    mid_ref[:group, :group] = real
    mid_ref[:group, group:] = -imag
    mid_ref[group:, :group] = imag
    mid_ref[group:, group:] = real

    number = lax.broadcasted_iota(jnp.int32, (size, size), 0)
    lows = []
    for k in range(2):
        pick = pick_rows(low_order_ref, k, number, (size, size))
        lows.append([permuted(low_gates_ref[k, c], pick) for c in range(2)])
    (right_re, right_im), (left_re, left_im) = lows
    real = (dot(left_re, right_re) - dot(left_im, right_im)).T
    imag = (dot(left_re, right_im) + dot(left_im, right_re)).T
    low_ref[:size, :size] = real
    low_ref[:size, size:] = imag
    low_ref[size:, :size] = -imag
    low_ref[size:, size:] = real


def core_factor(unit_ref, other):
    core = core_of()
    source = 1 - core if other else core
    return tuple(unit_ref[pl.ds(c * 4 + core * 2 + source, 1), :] for c in range(2))


def own_kernel(unit_ref, mine_ref, out_ref):
    re, im = core_factor(unit_ref, False)
    half = mine_ref.shape[1]
    out_ref[pl.ds(0, half, 2), :] = re * mine_ref[0] - im * mine_ref[1]
    out_ref[pl.ds(1, half, 2), :] = re * mine_ref[1] + im * mine_ref[0]


def first_kernel(unit_ref, own_ref, other_ref, out_ref):
    re, im = core_factor(unit_ref, True)
    half = other_ref.shape[1]
    for c, add in (
        (0, re * other_ref[0] - im * other_ref[1]),
        (1, re * other_ref[1] + im * other_ref[0]),
    ):
        out_ref[pl.ds(c, half, 2), :] = own_ref[pl.ds(c, half, 2), :] + add


def middle_kernel(moved_ref, mid_ref, low_ref, out_ref):
    rows, order = moved_ref.shape
    size = rows // 4

    def place(pair, c):
        return pl.ds(pair * 2 + c, size, 4)

    stacked = jnp.concatenate(
        [
            jnp.concatenate([moved_ref[place(pair, c), :] for pair in range(2)], axis=1)
            for c in range(2)
        ],
        axis=0,
    )
    mixed = dot3(mid_ref[...], stacked)
    turned = jnp.concatenate(
        [
            jnp.concatenate(
                [
                    mixed[c * size : (c + 1) * size, pair * order : (pair + 1) * order]
                    for c in range(2)
                ],
                axis=1,
            )
            for pair in range(2)
        ],
        axis=0,
    )
    last = dot3(turned, low_ref[...])
    for pair in range(2):
        for c in range(2):
            out_ref[place(pair, c), :] = last[
                pair * size : (pair + 1) * size, c * order : (c + 1) * order
            ]


def last_kernel(rows_ref, out_ref):
    half = out_ref.shape[1]
    for c in range(2):
        out_ref[c] = rows_ref[pl.ds(c, half, 2), :]


def call(kernel, shapes, *operands, specs=None):
    out = jax.tree.map(
        lambda shape: jax.ShapeDtypeStruct(shape, jnp.float32),
        shapes,
        is_leaf=lambda shape: isinstance(shape, tuple),
    )
    return pl.pallas_call(
        kernel,
        out_shape=out,
        in_specs=specs or [IN_VMEM] * len(operands),
        out_specs=jax.tree.map(lambda _: IN_VMEM, out),
        compiler_params=pltpu.CompilerParams(vmem_limit_bytes=32 * 2**20),
    )(*operands)


def exchange(rows, stages):
    blocks = rows.reshape(16, 64, -1)
    blocks = lax.all_to_all(blocks, AXIS, 0, 0, axis_index_groups=stages[0], tiled=True)
    blocks = blocks.reshape(16, 16, 4, -1).transpose(1, 0, 2, 3).reshape(16, 64, -1)
    blocks = lax.all_to_all(blocks, AXIS, 0, 0, axis_index_groups=stages[1], tiled=True)
    return blocks.reshape(rows.shape)


def body(state, low_gates, low_order, high_gates, mid_gate, mid_order):
    order = state.shape[3]
    pairs = state.shape[1] * state.shape[2]
    rows = (2 * pairs, order)

    mine = state.reshape(2, pairs, order)
    other = lax.ppermute(mine, AXIS, [(number, number ^ 128) for number in range(512)])
    units = jnp.broadcast_to(high_gates.reshape(16, 1), (16, order))
    own = call(own_kernel, rows, units, mine)
    sent = call(first_kernel, rows, units, own, other)
    sent, low_gates, low_order, mid_gate, mid_order = lax.optimization_barrier(
        (sent, low_gates, low_order, mid_gate, mid_order)
    )
    moved = exchange(sent, STAGES)
    mid, low = call(
        gates_kernel,
        [(4 * order, 4 * order), (2 * order, 2 * order)],
        low_order,
        mid_order.reshape(1, -1),
        units,
        low_gates,
        mid_gate,
        specs=[IN_SMEM] * 2 + [IN_VMEM] * 3,
    )
    done = call(middle_kernel, rows, moved, mid, low)
    back = exchange(done, STAGES[::-1])
    return call(last_kernel, (2, pairs, order), back).reshape(state.shape)


def solution(mesh):
    return jax.shard_map(
        body,
        mesh=Mesh(mesh.devices.reshape(-1), (AXIS,)),
        in_specs=(P(None, AXIS, None, None), P(), P(), P(), P(), P()),
        out_specs=P(None, AXIS, None, None),
        check_vma=False,
    )
```

time: 99.3 us -> 97.4 us (0.981)
  the two profiles are of different devices: /device:TPU:2 before, /device:TPU:32 now
where the time goes in v5:
time: 97.4 us; the launch traced here: 96.9 us
  blocking collectives  72.2 us (74%)
  starting transfers between devices  9.28 us (10%)
  waiting for transfers between devices  6.31 us (6%)
  Pallas kernels  5.51 us (6%)
  local copies, waits for them, and re-layouts  3.6 us (4%)
    all_to_all x2, blocking collectives, exchange(): lax.all_to_all(blocks, AXIS, 0, 0, axis_index_groups=stages[0], tiled=True)  47 us
    all_to_all x1, blocking collectives, exchange(): lax.all_to_all(blocks, AXIS, 0, 0, axis_index_groups=stages[1], tiled=True)  25.2 us
    all_to_all x1, starting transfers between devices, exchange(): lax.all_to_all(blocks, AXIS, 0, 0, axis_index_groups=stages[1], tiled=True)  7.37 us
    all_to_all x1, waiting for transfers between devices, exchange(): lax.all_to_all(blocks, AXIS, 0, 0, axis_index_groups=stages[1], tiled=True)  6.19 us
    pallas_call x5, Pallas kernels, call(): pl.pallas_call(kernel, out_shape=out, in_specs=specs or [IN_VMEM] * len(o...  5.51 us
  transfers between devices with their start and end apart: 2, of which 2 were waited for; matrix products, arithmetic and copies ran while one was open for 1% of the time, Pallas kernels for 3%

profile of v5, /device:TPU:32, one launch (start us, length us, event | category | flops | bytes accessed | tf_op | source)
XLA Modules:
  0.0 96.9 jit_solution(17311761592552724069)
XLA Ops:
  0.0 1.9 %collective-permute-start = (f32[2,512,128]{2,1,0:T(8,128)}, f32[2,512,128]{2,1,0:T(8,128)S(1)}, u32[]{:S(2)}, u32[]{:S(2)}) collective-permute-start(f32[2,512,128]{2,1,0:T(8,128)} %bitcast.19), channel_id=1, source_target_pairs={{0,128},{1,129},{2,130},{3,131},{4,132},{5,133},{6,134},{7,135},{8... | collective-permute-start | bytes 1572872 | tf_op jit(solution)/shard_map/ppermute | solution.py:201
  1.9 0.8 broadcast_in_dim.7
  2.7 0.1 broadcast_in_dim.8.unit_ref
  2.8 0.0 copy-start
  2.8 1.0 %copy-done = f32[2,4,128,128]{3,2,1,0:T(8,128)S(1)} copy-done((f32[2,4,128,128]{3,2,1,0:T(8,128)S(1)}, f32[2,4,128,128]{3,2,1,0:T(8,128)}, u32[]{:S(2)}) %copy-start) | copy-done | bytes 524312
  3.8 0.1 shard_map.64.own_ref
  3.9 0.1 collective-permute-done.other_ref
  4.0 0.1 shard_map.65
  4.1 33.9 %all_to_all.20 = f32[16,64,128]{2,1,0:T(8,128)S(1)} all-to-all(f32[16,64,128]{2,1,0:T(8,128)S(1)} %bitcast.15), channel_id=1, replica_groups={{0,4,8,12,16,20,24,28,256,260,264,268,272,276,280,284},{1,5,9,13,17,21,..., dimensions={0} | all-to-all | bytes 1048576 | tf_op jit(solution)/shard_map/all_to_all | solution.py:189
  38.0 0.9 copy.7
  39.0 0.0 copy-start.1
  39.0 0.0 copy-start.2
  39.0 7.4 %all-to-all-start.1 = ((f32[16,64,128]{2,1,0:T(8,128)}), f32[16,64,128]{2,1,0:T(8,128)S(1)}, u32[]{:S(2)}, u32[]{:S(2)}) async-start(f32[16,64,128]{2,1,0:T(8,128)} %bitcast.4), calls=%async_computation.1 | async-start | bytes 1048576 | tf_op jit(solution)/shard_map/all_to_all | solution.py:191
  46.4 0.0 copy-start.3
  46.4 0.0 copy-start.4
  46.4 0.0 copy-done.1
  46.4 0.0 copy-done.2
  46.4 0.6 copy-done.3
  47.0 0.0 copy-done.4
  47.0 3.3 %shard_map.66 = (f32[512,512]{1,0:T(8,128)S(1)}, f32[256,256]{1,0:T(8,128)S(1)}) custom-call(s32[2,7]{1,0:T(2,128)S(1)} %copy-done.3, s32[1,7]{1,0:T(1,128)S(1)} %bitcast.21, f32[16,128]{1,0:T(8,128)S(1)} %broadcast_in_dim.8.unit_ref, f32[2,2,128,128]{3,2,1,0:T(8,128)S(1)} %copy-done.1, f32[2,128,128]{2,1,0:T(8,128)S(1)} %copy-done.2), custom_call_target="tpu_custom_call" | custom-call | tf_op jit(solution)/shard_map/pallas_call | solution.py:178
  50.3 6.2 %all-to-all-done.1 = f32[16,64,128]{2,1,0:T(8,128)S(1)} async-done(((f32[16,64,128]{2,1,0:T(8,128)}), f32[16,64,128]{2,1,0:T(8,128)S(1)}, u32[]{:S(2)}, u32[]{:S(2)}) %all-to-all-start.1) | async-done | bytes 524320 | tf_op jit(solution)/shard_map/all_to_all | solution.py:191
  56.5 1.2 %shard_map.67 = f32[1024,128]{1,0:T(8,128)S(1)} custom-call(f32[1024,128]{1,0:T(8,128)S(1)} %bitcast.17, f32[512,512]{1,0:T(8,128)S(1)} %get-tuple-element.17.mid_ref, f32[256,256]{1,0:T(8,128)S(1)} %get-tuple-element.18.low_ref), custom_call_target="tpu_custom_call" | custom-call | tf_op jit(solution)/shard_map/pallas_call | solution.py:178
  57.7 13.1 %all_to_all.21 = f32[16,64,128]{2,1,0:T(8,128)S(1)} all-to-all(f32[16,64,128]{2,1,0:T(8,128)S(1)} %bitcast.18), channel_id=1, replica_groups={{0,1,2,3,32,33,34,35,64,65,66,67,96,97,98,99},{4,5,6,7,36,37,38,39,68,6..., dimensions={0} | all-to-all | bytes 1048576 | tf_op jit(solution)/shard_map/all_to_all | solution.py:189
  70.8 0.1 copy.8
  70.9 25.2 %all_to_all.22 = f32[16,64,128]{2,1,0:T(8,128)S(1)} all-to-all(f32[16,64,128]{2,1,0:T(8,128)S(1)} %bitcast.24), channel_id=1, replica_groups={{0,4,8,12,16,20,24,28,256,260,264,268,272,276,280,284},{1,5,9,13,17,21,..., dimensions={0} | all-to-all | bytes 1048576 | tf_op jit(solution)/shard_map/all_to_all | solution.py:191
  96.1 0.8 shard_map.68
Async XLA Ops:
  0.0 4.0 %collective-permute-start = (f32[2,512,128]{2,1,0:T(8,128)}, f32[2,512,128]{2,1,0:T(8,128)S(1)}, u32[]{:S(2)}, u32[]{:S(2)}) collective-permute-start(f32[2,512,128]{2,1,0:T(8,128)} %bitcast.19), channel_id=1, source_target_pairs={{0,128},{1,129},{2,130},{3,131},{4,132},{5,133},{6,134},{7,135},{8... | collective-permute-start | bytes 1572872 | tf_op jit(solution)/shard_map/ppermute | solution.py:201
  2.8 1.0 %copy-start = (f32[2,4,128,128]{3,2,1,0:T(8,128)S(1)}, f32[2,4,128,128]{3,2,1,0:T(8,128)}, u32[]{:S(2)}) copy-start(f32[2,4,128,128]{3,2,1,0:T(8,128)} %param.6) | copy-start | bytes 1572868
  39.0 7.4 %copy-start.1 = (f32[2,2,128,128]{3,2,1,0:T(8,128)S(1)}, f32[2,2,128,128]{3,2,1,0:T(8,128)}, u32[]{:S(2)}) copy-start(f32[2,2,128,128]{3,2,1,0:T(8,128)} %low_gates_ref) | copy-start | bytes 786436
  39.0 7.4 %copy-start.2 = (f32[2,128,128]{2,1,0:T(8,128)S(1)}, f32[2,128,128]{2,1,0:T(8,128)}, u32[]{:S(2)}) copy-start(f32[2,128,128]{2,1,0:T(8,128)} %mid_gate_ref) | copy-start | bytes 393220
  39.0 17.5 %all-to-all-start.1 = ((f32[16,64,128]{2,1,0:T(8,128)}), f32[16,64,128]{2,1,0:T(8,128)S(1)}, u32[]{:S(2)}, u32[]{:S(2)}) async-start(f32[16,64,128]{2,1,0:T(8,128)} %bitcast.4), calls=%async_computation.1 | async-start | bytes 1048576 | tf_op jit(solution)/shard_map/all_to_all | solution.py:191
  46.4 0.7 copy-start.3
  46.4 0.7 copy-start.4

commit v6 on v5

--- a/solution.py
+++ b/solution.py
@@ -10,7 +10,8 @@
 AXIS = "device"
 NUMBERS = np.arange(512).reshape(2, 2, 4, 8, 4).transpose(1, 0, 3, 2, 4).reshape(2, 16, 16)
 LINES = [[group.tolist() for group in NUMBERS[core].T] for core in range(2)]
-PLANES = [[group.tolist() for group in NUMBERS[core]] for core in range(2)]
+PLACES = [k ^ k >> 2 for k in range(16)]
+PLANES = [[group[PLACES].tolist() for group in NUMBERS[core]] for core in range(2)]
 STAGES = (LINES[0] + PLANES[1], PLANES[0] + LINES[1])
 HIGHEST = lax.Precision.HIGHEST
 IN_VMEM = pl.BlockSpec(memory_space=pltpu.VMEM)
@@ -22,12 +23,40 @@
     return top, (value - top.astype(jnp.float32)).astype(jnp.bfloat16)
 
 
+def bf16_dot(left, right):
+    return jnp.dot(left, right, preferred_element_type=jnp.float32)
+
+
 def dot3(left, right):
-    def prod(a, b):
-        return jnp.dot(a, b, preferred_element_type=jnp.float32)
-
-    (left_top, left_rest), (right_top, right_rest) = split(left), split(right)
-    return prod(left_top, right_rest) + prod(left_rest, right_top) + prod(left_top, right_top)
+    return (
+        bf16_dot(left[0], right[1]) + bf16_dot(left[1], right[0]) + bf16_dot(left[0], right[0])
+    )
+
+
+def pick_dot(left, right):
+    on_left = left.dtype == jnp.bfloat16
+    value = right if on_left else left
+    total = None
+    for _ in range(3):
+        part = value.astype(jnp.bfloat16)
+        value = value - part.astype(jnp.float32)
+        term = (
+            bf16_dot(left, part)
+            if on_left
+            else lax.dot_general(
+                part, right, (((1,), (1,)), ((), ())), preferred_element_type=jnp.float32
+            )
+        )
+        total = term if total is None else total + term
+    return total
+
+
+def store_split(ref, *quarters):
+    size = quarters[0].shape[0]
+    for at, quarter in enumerate(quarters):
+        rows, columns = (pl.ds(place * size, size) for place in (at // 2, at % 2))
+        for part, value in enumerate(split(quarter)):
+            ref[part, rows, columns] = value
 
 
 def core_of():
@@ -50,24 +79,21 @@
 
     def parts(number):
         plane = jnp.where(lines, number >> 4, number & 15)
+        plane = plane ^ plane >> 2
         line = jnp.where(lines, number & 15, number >> 4)
         return line >> 3, (plane >> 2) << 5 | (line & 7) << 2 | plane & 3
 
-    def dot(left, right):
-        return jnp.dot(left, right, precision=HIGHEST, preferred_element_type=jnp.float32)
-
     def permuted(gate, pick):
-        return lax.dot_general(
-            dot(pick, gate),
-            pick,
-            (((1,), (1,)), ((), ())),
-            precision=HIGHEST,
-            preferred_element_type=jnp.float32,
-        )
+        chosen = pick.astype(jnp.bfloat16)
+        half = pick_dot(chosen, jnp.concatenate([gate[0], gate[1]], axis=1))
+        count = gate.shape[2]
+        stacked = jnp.concatenate([half[:, :count], half[:, count:]], axis=0)
+        whole = pick_dot(stacked, chosen)
+        return whole[: pick.shape[0]], whole[pick.shape[0] :]
 
     into, index = parts(lax.broadcasted_iota(jnp.int32, (group, size), 0))
     pick = pick_rows(mid_order_ref, 0, index, (group, size))
-    mid_re, mid_im = (permuted(mid_gate_ref[c], pick) for c in range(2))
+    mid_re, mid_im = permuted(mid_gate_ref, pick)
     into, _ = parts(lax.broadcasted_iota(jnp.int32, (group, group), 0))
     source, _ = parts(lax.broadcasted_iota(jnp.int32, (group, group), 1))
 
@@ -85,23 +111,28 @@
     unit_re, unit_im = factor(0), factor(1)
     real = unit_re * mid_re - unit_im * mid_im
     imag = unit_re * mid_im + unit_im * mid_re
-    mid_ref[:group, :group] = real
-    mid_ref[:group, group:] = -imag
-    mid_ref[group:, :group] = imag
-    mid_ref[group:, group:] = real
+    store_split(mid_ref, real, -imag, imag, real)
 
     number = lax.broadcasted_iota(jnp.int32, (size, size), 0)
-    lows = []
-    for k in range(2):
-        pick = pick_rows(low_order_ref, k, number, (size, size))
-        lows.append([permuted(low_gates_ref[k, c], pick) for c in range(2)])
-    (right_re, right_im), (left_re, left_im) = lows
-    real = (dot(left_re, right_re) - dot(left_im, right_im)).T
-    imag = (dot(left_re, right_im) + dot(left_im, right_re)).T
-    low_ref[:size, :size] = real
-    low_ref[:size, size:] = imag
-    low_ref[size:, :size] = -imag
-    low_ref[size:, size:] = real
+    right, left = (
+        permuted(low_gates_ref[k], pick_rows(low_order_ref, k, number, (size, size)))
+        for k in range(2)
+    )
+    left = jnp.concatenate(
+        [
+            jnp.concatenate([left[0], -left[1]], axis=1),
+            jnp.concatenate([left[1], left[0]], axis=1),
+        ],
+        axis=0,
+    )
+    both = jnp.dot(
+        left,
+        jnp.concatenate(right, axis=0),
+        precision=HIGHEST,
+        preferred_element_type=jnp.float32,
+    )
+    real, imag = both[:size].T, both[size:].T
+    store_split(low_ref, real, imag, -imag, real)
 
 
 def core_factor(unit_ref, other):
@@ -141,7 +172,7 @@
         ],
         axis=0,
     )
-    mixed = dot3(mid_ref[...], stacked)
+    mixed = dot3((mid_ref[0], mid_ref[1]), split(stacked))
     turned = jnp.concatenate(
         [
             jnp.concatenate(
@@ -155,7 +186,7 @@
         ],
         axis=0,
     )
-    last = dot3(turned, low_ref[...])
+    last = dot3(split(turned), (low_ref[0], low_ref[1]))
     for pair in range(2):
         for c in range(2):
             out_ref[place(pair, c), :] = last[
@@ -169,12 +200,7 @@
         out_ref[c] = rows_ref[pl.ds(c, half, 2), :]
 
 
-def call(kernel, shapes, *operands, specs=None):
-    out = jax.tree.map(
-        lambda shape: jax.ShapeDtypeStruct(shape, jnp.float32),
-        shapes,
-        is_leaf=lambda shape: isinstance(shape, tuple),
-    )
+def call(kernel, out, *operands, specs=None):
     return pl.pallas_call(
         kernel,
         out_shape=out,
@@ -195,20 +221,20 @@
 def body(state, low_gates, low_order, high_gates, mid_gate, mid_order):
     order = state.shape[3]
     pairs = state.shape[1] * state.shape[2]
-    rows = (2 * pairs, order)
+    rows = jax.ShapeDtypeStruct((2 * pairs, order), jnp.float32)
 
     mine = state.reshape(2, pairs, order)
     other = lax.ppermute(mine, AXIS, [(number, number ^ 128) for number in range(512)])
     units = jnp.broadcast_to(high_gates.reshape(16, 1), (16, order))
     own = call(own_kernel, rows, units, mine)
     sent = call(first_kernel, rows, units, own, other)
-    sent, low_gates, low_order, mid_gate, mid_order = lax.optimization_barrier(
-        (sent, low_gates, low_order, mid_gate, mid_order)
-    )
     moved = exchange(sent, STAGES)
     mid, low = call(
         gates_kernel,
-        [(4 * order, 4 * order), (2 * order, 2 * order)],
+        [
+            jax.ShapeDtypeStruct((2, size * order, size * order), jnp.bfloat16)
+            for size in (4, 2)
+        ],
         low_order,
         mid_order.reshape(1, -1),
         units,
@@ -218,7 +244,8 @@
     )
     done = call(middle_kernel, rows, moved, mid, low)
     back = exchange(done, STAGES[::-1])
-    return call(last_kernel, (2, pairs, order), back).reshape(state.shape)
+    final = jax.ShapeDtypeStruct(mine.shape, jnp.float32)
+    return call(last_kernel, final, back).reshape(state.shape)
 
 
 def solution(mesh):

time: 97.4 us -> 96.7 us (level)
  transfers between devices with their start and end apart: 2 -> 2, of which waited for: 2 -> 2; matrix products, arithmetic and copies ran while one was open for 1% -> 1% of each run, Pallas kernels for 3% -> 2%
where the time goes in v6:
time: 96.7 us; the launch traced here: 96.3 us
  blocking collectives  72.1 us (75%)
  starting transfers between devices  9.25 us (10%)
  waiting for transfers between devices  6.72 us (7%)
  Pallas kernels  4.54 us (5%)
  local copies, waits for them, and re-layouts  3.6 us (4%)
    all_to_all x2, blocking collectives, exchange(): lax.all_to_all(blocks, AXIS, 0, 0, axis_index_groups=stages[0], tiled=True)  46.9 us
    all_to_all x1, blocking collectives, exchange(): lax.all_to_all(blocks, AXIS, 0, 0, axis_index_groups=stages[1], tiled=True)  25.2 us
    all_to_all x1, starting transfers between devices, exchange(): lax.all_to_all(blocks, AXIS, 0, 0, axis_index_groups=stages[1], tiled=True)  7.34 us
    all_to_all x1, waiting for transfers between devices, exchange(): lax.all_to_all(blocks, AXIS, 0, 0, axis_index_groups=stages[1], tiled=True)  6.6 us
    pallas_call x5, Pallas kernels, call(): pl.pallas_call(kernel, out_shape=out, in_specs=specs or [IN_VMEM] * len(o...  4.54 us
  transfers between devices with their start and end apart: 2, of which 2 were waited for; matrix products, arithmetic and copies ran while one was open for 1% of the time, Pallas kernels for 2%

profile of v6, /device:TPU:32, one launch (start us, length us, event | category | flops | bytes accessed | tf_op | source)
XLA Modules:
  0.0 96.3 jit_solution(12229842074580423078)
XLA Ops:
  0.0 1.9 %collective-permute-start = (f32[2,512,128]{2,1,0:T(8,128)}, f32[2,512,128]{2,1,0:T(8,128)S(1)}, u32[]{:S(2)}, u32[]{:S(2)}) collective-permute-start(f32[2,512,128]{2,1,0:T(8,128)} %bitcast.19), channel_id=1, source_target_pairs={{0,128},{1,129},{2,130},{3,131},{4,132},{5,133},{6,134},{7,135},{8... | collective-permute-start | bytes 1572872 | tf_op jit(solution)/shard_map/ppermute | solution.py:227
  1.9 0.8 broadcast_in_dim.7
  2.7 0.1 broadcast_in_dim.8.unit_ref
  2.8 0.0 copy-start
  2.8 1.0 %copy-done = f32[2,4,128,128]{3,2,1,0:T(8,128)S(1)} copy-done((f32[2,4,128,128]{3,2,1,0:T(8,128)S(1)}, f32[2,4,128,128]{3,2,1,0:T(8,128)}, u32[]{:S(2)}) %copy-start) | copy-done | bytes 524312
  3.8 0.1 shard_map.64.own_ref
  3.9 0.1 collective-permute-done.other_ref
  4.0 0.1 shard_map.65
  4.1 33.9 %all_to_all.20 = f32[16,64,128]{2,1,0:T(8,128)S(1)} all-to-all(f32[16,64,128]{2,1,0:T(8,128)S(1)} %bitcast.15), channel_id=1, replica_groups={{0,4,8,12,16,20,24,28,256,260,264,268,272,276,280,284},{1,5,9,13,17,21,..., dimensions={0} | all-to-all | bytes 1048576 | tf_op jit(solution)/shard_map/all_to_all | solution.py:215
  38.1 0.9 copy.7
  39.0 0.0 copy-start.1
  39.0 0.0 copy-start.2
  39.0 7.3 %all-to-all-start.1 = ((f32[16,64,128]{2,1,0:T(8,128)}), f32[16,64,128]{2,1,0:T(8,128)S(1)}, u32[]{:S(2)}, u32[]{:S(2)}) async-start(f32[16,64,128]{2,1,0:T(8,128)} %bitcast.4), calls=%async_computation.1 | async-start | bytes 1048576 | tf_op jit(solution)/shard_map/all_to_all | solution.py:217
  46.4 0.0 copy-start.3
  46.4 0.0 copy-start.4
  46.4 0.0 copy-done.1
  46.4 0.0 copy-done.2
  46.4 0.6 copy-done.3
  47.0 0.0 copy-done.4
  47.0 2.3 %shard_map.66 = (bf16[2,512,512]{2,1,0:T(8,128)(2,1)S(1)}, bf16[2,256,256]{2,1,0:T(8,128)(2,1)S(1)}) custom-call(s32[2,7]{1,0:T(2,128)S(1)} %copy-done.3, s32[1,7]{1,0:T(1,128)S(1)} %bitcast.21, f32[16,128]{1,0:T(8,128)S(1)} %broadcast_in_dim.8.unit_ref, f32[2,2,128,128]{3,2,1,0:T(8,128)S(1)} %copy-done.1, f32[2,128,128]{2,1,0:T(8,128)S(1)} %copy-done.2), custom_call_target="tpu_custom_call" | custom-call | tf_op jit(solution)/shard_map/pallas_call | solution.py:204
  49.3 6.6 %all-to-all-done.1 = f32[16,64,128]{2,1,0:T(8,128)S(1)} async-done(((f32[16,64,128]{2,1,0:T(8,128)}), f32[16,64,128]{2,1,0:T(8,128)S(1)}, u32[]{:S(2)}, u32[]{:S(2)}) %all-to-all-start.1) | async-done | bytes 524320 | tf_op jit(solution)/shard_map/all_to_all | solution.py:217
  55.9 1.2 %shard_map.67 = f32[1024,128]{1,0:T(8,128)S(1)} custom-call(f32[1024,128]{1,0:T(8,128)S(1)} %bitcast.17, bf16[2,512,512]{2,1,0:T(8,128)(2,1)S(1)} %get-tuple-element.7.mid_ref, bf16[2,256,256]{2,1,0:T(8,128)(2,1)S(1)} %get-tuple-element.8.low_ref), custom_call_target="tpu_custom_call" | custom-call | tf_op jit(solution)/shard_map/pallas_call | solution.py:204
  57.2 13.0 %all_to_all.21 = f32[16,64,128]{2,1,0:T(8,128)S(1)} all-to-all(f32[16,64,128]{2,1,0:T(8,128)S(1)} %bitcast.18), channel_id=1, replica_groups={{0,1,2,3,33,32,35,34,66,67,64,65,99,98,97,96},{4,5,6,7,37,36,39,38,70,7..., dimensions={0} | all-to-all | bytes 1048576 | tf_op jit(solution)/shard_map/all_to_all | solution.py:215
  70.2 0.1 copy.8
  70.3 25.2 %all_to_all.22 = f32[16,64,128]{2,1,0:T(8,128)S(1)} all-to-all(f32[16,64,128]{2,1,0:T(8,128)S(1)} %bitcast.24), channel_id=1, replica_groups={{0,4,8,12,16,20,24,28,256,260,264,268,272,276,280,284},{1,5,9,13,17,21,..., dimensions={0} | all-to-all | bytes 1048576 | tf_op jit(solution)/shard_map/all_to_all | solution.py:217
  95.5 0.8 shard_map.68
Async XLA Ops:
  0.0 4.0 %collective-permute-start = (f32[2,512,128]{2,1,0:T(8,128)}, f32[2,512,128]{2,1,0:T(8,128)S(1)}, u32[]{:S(2)}, u32[]{:S(2)}) collective-permute-start(f32[2,512,128]{2,1,0:T(8,128)} %bitcast.19), channel_id=1, source_target_pairs={{0,128},{1,129},{2,130},{3,131},{4,132},{5,133},{6,134},{7,135},{8... | collective-permute-start | bytes 1572872 | tf_op jit(solution)/shard_map/ppermute | solution.py:227
  2.8 1.0 %copy-start = (f32[2,4,128,128]{3,2,1,0:T(8,128)S(1)}, f32[2,4,128,128]{3,2,1,0:T(8,128)}, u32[]{:S(2)}) copy-start(f32[2,4,128,128]{3,2,1,0:T(8,128)} %param.6) | copy-start | bytes 1572868
  39.0 7.4 %copy-start.1 = (f32[2,2,128,128]{3,2,1,0:T(8,128)S(1)}, f32[2,2,128,128]{3,2,1,0:T(8,128)}, u32[]{:S(2)}) copy-start(f32[2,2,128,128]{3,2,1,0:T(8,128)} %low_gates_ref.1) | copy-start | bytes 786436
  39.0 7.4 %copy-start.2 = (f32[2,128,128]{2,1,0:T(8,128)S(1)}, f32[2,128,128]{2,1,0:T(8,128)}, u32[]{:S(2)}) copy-start(f32[2,128,128]{2,1,0:T(8,128)} %mid_gate_ref.1) | copy-start | bytes 393220
  39.0 16.9 %all-to-all-start.1 = ((f32[16,64,128]{2,1,0:T(8,128)}), f32[16,64,128]{2,1,0:T(8,128)S(1)}, u32[]{:S(2)}, u32[]{:S(2)}) async-start(f32[16,64,128]{2,1,0:T(8,128)} %bitcast.4), calls=%async_computation.1 | async-start | bytes 1048576 | tf_op jit(solution)/shard_map/all_to_all | solution.py:217
  46.4 0.7 copy-start.3
  46.4 0.7 copy-start.4

commit v7 on v6

--- a/solution.py
+++ b/solution.py
@@ -13,9 +13,8 @@
 PLACES = [k ^ k >> 2 for k in range(16)]
 PLANES = [[group[PLACES].tolist() for group in NUMBERS[core]] for core in range(2)]
 STAGES = (LINES[0] + PLANES[1], PLANES[0] + LINES[1])
-HIGHEST = lax.Precision.HIGHEST
+REPEATS = 13
 IN_VMEM = pl.BlockSpec(memory_space=pltpu.VMEM)
-IN_SMEM = pl.BlockSpec(memory_space=pltpu.SMEM)
 
 
 def split(value):
@@ -66,7 +65,7 @@
 def pick_rows(order_ref, at, number, columns):
     where = jnp.zeros_like(number)
     for j in range(order_ref.shape[1]):
-        where += (number >> j & 1) << order_ref[at, j]
+        where += (number >> j & 1) << order_ref[at : at + 1, j : j + 1]
     return (where == lax.broadcasted_iota(jnp.int32, columns, 1)).astype(jnp.float32)
 
 
@@ -125,12 +124,7 @@
         ],
         axis=0,
     )
-    both = jnp.dot(
-        left,
-        jnp.concatenate(right, axis=0),
-        precision=HIGHEST,
-        preferred_element_type=jnp.float32,
-    )
+    both = dot3(split(left), split(jnp.concatenate(right, axis=0)))
     real, imag = both[:size].T, both[size:].T
     store_split(low_ref, real, imag, -imag, real)
 
@@ -151,11 +145,16 @@
 def first_kernel(unit_ref, own_ref, other_ref, out_ref):
     re, im = core_factor(unit_ref, True)
     half = other_ref.shape[1]
-    for c, add in (
-        (0, re * other_ref[0] - im * other_ref[1]),
-        (1, re * other_ref[1] + im * other_ref[0]),
-    ):
-        out_ref[pl.ds(c, half, 2), :] = own_ref[pl.ds(c, half, 2), :] + add
+
+    def store(_, carry):
+        for c, add in (
+            (0, re * other_ref[0] - im * other_ref[1]),
+            (1, re * other_ref[1] + im * other_ref[0]),
+        ):
+            out_ref[pl.ds(c, half, 2), :] = own_ref[pl.ds(c, half, 2), :] + add
+        return carry
+
+    lax.fori_loop(0, 1 + REPEATS * core_of(), store, 0)
 
 
 def middle_kernel(moved_ref, mid_ref, low_ref, out_ref):
@@ -200,11 +199,11 @@
         out_ref[c] = rows_ref[pl.ds(c, half, 2), :]
 
 
-def call(kernel, out, *operands, specs=None):
+def call(kernel, out, *operands):
     return pl.pallas_call(
         kernel,
         out_shape=out,
-        in_specs=specs or [IN_VMEM] * len(operands),
+        in_specs=[IN_VMEM] * len(operands),
         out_specs=jax.tree.map(lambda _: IN_VMEM, out),
         compiler_params=pltpu.CompilerParams(vmem_limit_bytes=32 * 2**20),
     )(*operands)
@@ -227,8 +226,6 @@
     other = lax.ppermute(mine, AXIS, [(number, number ^ 128) for number in range(512)])
     units = jnp.broadcast_to(high_gates.reshape(16, 1), (16, order))
     own = call(own_kernel, rows, units, mine)
-    sent = call(first_kernel, rows, units, own, other)
-    moved = exchange(sent, STAGES)
     mid, low = call(
         gates_kernel,
         [
@@ -240,8 +237,9 @@
         units,
         low_gates,
         mid_gate,
-        specs=[IN_SMEM] * 2 + [IN_VMEM] * 3,
-    )
+    )
+    sent = call(first_kernel, rows, units, own, other)
+    moved = exchange(sent, STAGES)
     done = call(middle_kernel, rows, moved, mid, low)
     back = exchange(done, STAGES[::-1])
     final = jax.ShapeDtypeStruct(mine.shape, jnp.float32)

time: 96.7 us -> 96.6 us (level)
  no operation moved by 1% of the time
where the time goes in v7:
time: 96.6 us; the launch traced here: 96.2 us
  blocking collectives  71.9 us (74%)
  starting transfers between devices  9.37 us (10%)
  waiting for transfers between devices  7.46 us (8%)
  Pallas kernels  3.8 us (4%)
  local copies, waits for them, and re-layouts  3.6 us (4%)
    all_to_all x2, blocking collectives, exchange(): lax.all_to_all(blocks, AXIS, 0, 0, axis_index_groups=stages[0], tiled=True)  46.9 us
    all_to_all x1, blocking collectives, exchange(): lax.all_to_all(blocks, AXIS, 0, 0, axis_index_groups=stages[1], tiled=True)  25 us
    all_to_all x1, starting transfers between devices, exchange(): lax.all_to_all(blocks, AXIS, 0, 0, axis_index_groups=stages[1], tiled=True)  7.46 us
    all_to_all x1, waiting for transfers between devices, exchange(): lax.all_to_all(blocks, AXIS, 0, 0, axis_index_groups=stages[1], tiled=True)  7.34 us
    pallas_call x5, Pallas kernels, call(): pl.pallas_call(kernel, out_shape=out, in_specs=[IN_VMEM] * len(operands),...  3.8 us
  transfers between devices with their start and end apart: 2, of which 2 were waited for; matrix products, arithmetic and copies ran while one was open for 1% of the time, Pallas kernels for 2%

profile of v7, /device:TPU:32, one launch (start us, length us, event | category | flops | bytes accessed | tf_op | source)
XLA Modules:
  0.0 96.2 jit_solution(3609490200908706769)
XLA Ops:
  0.0 1.9 %collective-permute-start = (f32[2,512,128]{2,1,0:T(8,128)}, f32[2,512,128]{2,1,0:T(8,128)S(1)}, u32[]{:S(2)}, u32[]{:S(2)}) collective-permute-start(f32[2,512,128]{2,1,0:T(8,128)} %bitcast.19), channel_id=1, source_target_pairs={{0,128},{1,129},{2,130},{3,131},{4,132},{5,133},{6,134},{7,135},{8... | collective-permute-start | bytes 1572872 | tf_op jit(solution)/shard_map/ppermute | solution.py:226
  1.9 0.8 broadcast_in_dim.7
  2.7 0.1 broadcast_in_dim.8.unit_ref
  2.8 0.0 copy-start
  2.8 1.0 %copy-done = f32[2,4,128,128]{3,2,1,0:T(8,128)S(1)} copy-done((f32[2,4,128,128]{3,2,1,0:T(8,128)S(1)}, f32[2,4,128,128]{3,2,1,0:T(8,128)}, u32[]{:S(2)}) %copy-start) | copy-done | bytes 524312
  3.8 0.1 shard_map.64.own_ref
  3.9 0.1 collective-permute-done.other_ref
  4.0 0.1 shard_map.65
  4.1 33.9 %all_to_all.20 = f32[16,64,128]{2,1,0:T(8,128)S(1)} all-to-all(f32[16,64,128]{2,1,0:T(8,128)S(1)} %bitcast.15), channel_id=1, replica_groups={{0,4,8,12,16,20,24,28,256,260,264,268,272,276,280,284},{1,5,9,13,17,21,..., dimensions={0} | all-to-all | bytes 1048576 | tf_op jit(solution)/shard_map/all_to_all | solution.py:214
  38.0 0.9 copy.7
  39.0 0.0 copy-start.1
  39.0 0.0 copy-start.2
  39.0 7.5 %all-to-all-start.1 = ((f32[16,64,128]{2,1,0:T(8,128)}), f32[16,64,128]{2,1,0:T(8,128)S(1)}, u32[]{:S(2)}, u32[]{:S(2)}) async-start(f32[16,64,128]{2,1,0:T(8,128)} %bitcast.4), calls=%async_computation.1 | async-start | bytes 1048576 | tf_op jit(solution)/shard_map/all_to_all | solution.py:216
  46.4 0.0 copy-start.3
  46.5 0.0 copy-start.4
  46.5 0.0 copy-done.1
  46.5 0.0 copy-done.2
  46.5 0.6 copy-done.3
  47.1 0.0 copy-done.4
  47.1 1.6 %shard_map.66 = (bf16[2,512,512]{2,1,0:T(8,128)(2,1)S(1)}, bf16[2,256,256]{2,1,0:T(8,128)(2,1)S(1)}) custom-call(s32[2,7]{1,0:T(2,128)S(1)} %copy-done.3, s32[1,7]{1,0:T(1,128)S(1)} %bitcast.21, f32[16,128]{1,0:T(8,128)S(1)} %broadcast_in_dim.8.unit_ref, f32[2,2,128,128]{3,2,1,0:T(8,128)S(1)} %copy-done.1, f32[2,128,128]{2,1,0:T(8,128)S(1)} %copy-done.2), custom_call_target="tpu_custom_call" | custom-call | tf_op jit(solution)/shard_map/pallas_call | solution.py:203
  48.7 7.3 %all-to-all-done.1 = f32[16,64,128]{2,1,0:T(8,128)S(1)} async-done(((f32[16,64,128]{2,1,0:T(8,128)}), f32[16,64,128]{2,1,0:T(8,128)S(1)}, u32[]{:S(2)}, u32[]{:S(2)}) %all-to-all-start.1) | async-done | bytes 524320 | tf_op jit(solution)/shard_map/all_to_all | solution.py:216
  56.0 1.2 %shard_map.67 = f32[1024,128]{1,0:T(8,128)S(1)} custom-call(f32[1024,128]{1,0:T(8,128)S(1)} %bitcast.17, bf16[2,512,512]{2,1,0:T(8,128)(2,1)S(1)} %get-tuple-element.7.mid_ref, bf16[2,256,256]{2,1,0:T(8,128)(2,1)S(1)} %get-tuple-element.8.low_ref), custom_call_target="tpu_custom_call" | custom-call | tf_op jit(solution)/shard_map/pallas_call | solution.py:203
  57.3 13.0 %all_to_all.21 = f32[16,64,128]{2,1,0:T(8,128)S(1)} all-to-all(f32[16,64,128]{2,1,0:T(8,128)S(1)} %bitcast.18), channel_id=1, replica_groups={{0,1,2,3,33,32,35,34,66,67,64,65,99,98,97,96},{4,5,6,7,37,36,39,38,70,7..., dimensions={0} | all-to-all | bytes 1048576 | tf_op jit(solution)/shard_map/all_to_all | solution.py:214
  70.2 0.1 copy.8
  70.4 25.0 %all_to_all.22 = f32[16,64,128]{2,1,0:T(8,128)S(1)} all-to-all(f32[16,64,128]{2,1,0:T(8,128)S(1)} %bitcast.24), channel_id=1, replica_groups={{0,4,8,12,16,20,24,28,256,260,264,268,272,276,280,284},{1,5,9,13,17,21,..., dimensions={0} | all-to-all | bytes 1048576 | tf_op jit(solution)/shard_map/all_to_all | solution.py:216
  95.4 0.8 shard_map.68
Async XLA Ops:
  0.0 4.0 %collective-permute-start = (f32[2,512,128]{2,1,0:T(8,128)}, f32[2,512,128]{2,1,0:T(8,128)S(1)}, u32[]{:S(2)}, u32[]{:S(2)}) collective-permute-start(f32[2,512,128]{2,1,0:T(8,128)} %bitcast.19), channel_id=1, source_target_pairs={{0,128},{1,129},{2,130},{3,131},{4,132},{5,133},{6,134},{7,135},{8... | collective-permute-start | bytes 1572872 | tf_op jit(solution)/shard_map/ppermute | solution.py:226
  2.8 1.0 %copy-start = (f32[2,4,128,128]{3,2,1,0:T(8,128)S(1)}, f32[2,4,128,128]{3,2,1,0:T(8,128)}, u32[]{:S(2)}) copy-start(f32[2,4,128,128]{3,2,1,0:T(8,128)} %param.6) | copy-start | bytes 1572868
  39.0 7.5 %copy-start.1 = (f32[2,2,128,128]{3,2,1,0:T(8,128)S(1)}, f32[2,2,128,128]{3,2,1,0:T(8,128)}, u32[]{:S(2)}) copy-start(f32[2,2,128,128]{3,2,1,0:T(8,128)} %low_gates_ref.1) | copy-start | bytes 786436
  39.0 7.5 %copy-start.2 = (f32[2,128,128]{2,1,0:T(8,128)S(1)}, f32[2,128,128]{2,1,0:T(8,128)}, u32[]{:S(2)}) copy-start(f32[2,128,128]{2,1,0:T(8,128)} %mid_gate_ref.1) | copy-start | bytes 393220
  39.0 17.1 %all-to-all-start.1 = ((f32[16,64,128]{2,1,0:T(8,128)}), f32[16,64,128]{2,1,0:T(8,128)S(1)}, u32[]{:S(2)}, u32[]{:S(2)}) async-start(f32[16,64,128]{2,1,0:T(8,128)} %bitcast.4), calls=%async_computation.1 | async-start | bytes 1048576 | tf_op jit(solution)/shard_map/all_to_all | solution.py:216
  46.4 0.7 copy-start.3
  46.5 0.7 copy-start.4

commit v8 on v7

--- a/solution.py
+++ b/solution.py
@@ -10,10 +10,9 @@
 AXIS = "device"
 NUMBERS = np.arange(512).reshape(2, 2, 4, 8, 4).transpose(1, 0, 3, 2, 4).reshape(2, 16, 16)
 LINES = [[group.tolist() for group in NUMBERS[core].T] for core in range(2)]
-PLACES = [k ^ k >> 2 for k in range(16)]
+PLACES = [k ^ (k >> 2 & 1) * 3 for k in range(16)]
 PLANES = [[group[PLACES].tolist() for group in NUMBERS[core]] for core in range(2)]
 STAGES = (LINES[0] + PLANES[1], PLANES[0] + LINES[1])
-REPEATS = 13
 IN_VMEM = pl.BlockSpec(memory_space=pltpu.VMEM)
 
 
@@ -78,7 +77,7 @@
 
     def parts(number):
         plane = jnp.where(lines, number >> 4, number & 15)
-        plane = plane ^ plane >> 2
+        plane = plane ^ (plane >> 2 & 1) * 3
         line = jnp.where(lines, number & 15, number >> 4)
         return line >> 3, (plane >> 2) << 5 | (line & 7) << 2 | plane & 3
 
@@ -145,16 +144,11 @@
 def first_kernel(unit_ref, own_ref, other_ref, out_ref):
     re, im = core_factor(unit_ref, True)
     half = other_ref.shape[1]
-
-    def store(_, carry):
-        for c, add in (
-            (0, re * other_ref[0] - im * other_ref[1]),
-            (1, re * other_ref[1] + im * other_ref[0]),
-        ):
-            out_ref[pl.ds(c, half, 2), :] = own_ref[pl.ds(c, half, 2), :] + add
-        return carry
-
-    lax.fori_loop(0, 1 + REPEATS * core_of(), store, 0)
+    for c, add in (
+        (0, re * other_ref[0] - im * other_ref[1]),
+        (1, re * other_ref[1] + im * other_ref[0]),
+    ):
+        out_ref[pl.ds(c, half, 2), :] = own_ref[pl.ds(c, half, 2), :] + add
 
 
 def middle_kernel(moved_ref, mid_ref, low_ref, out_ref):

time: 96.6 us -> 96.5 us (level)
  no operation moved by 1% of the time
where the time goes in v8:
time: 96.5 us; the launch traced here: 96.1 us
  blocking collectives  72.1 us (75%)
  starting transfers between devices  9.26 us (10%)
  waiting for transfers between devices  7.25 us (8%)
  Pallas kernels  3.81 us (4%)
  local copies, waits for them, and re-layouts  3.6 us (4%)
    all_to_all x2, blocking collectives, exchange(): lax.all_to_all(blocks, AXIS, 0, 0, axis_index_groups=stages[0], tiled=True)  46.9 us
    all_to_all x1, blocking collectives, exchange(): lax.all_to_all(blocks, AXIS, 0, 0, axis_index_groups=stages[1], tiled=True)  25.2 us
    all_to_all x1, starting transfers between devices, exchange(): lax.all_to_all(blocks, AXIS, 0, 0, axis_index_groups=stages[1], tiled=True)  7.35 us
    all_to_all x1, waiting for transfers between devices, exchange(): lax.all_to_all(blocks, AXIS, 0, 0, axis_index_groups=stages[1], tiled=True)  7.14 us
    pallas_call x5, Pallas kernels, call(): pl.pallas_call(kernel, out_shape=out, in_specs=[IN_VMEM] * len(operands),...  3.81 us
  transfers between devices with their start and end apart: 2, of which 2 were waited for; matrix products, arithmetic and copies ran while one was open for 1% of the time, Pallas kernels for 2%

profile of v8, /device:TPU:32, one launch (start us, length us, event | category | flops | bytes accessed | tf_op | source)
XLA Modules:
  0.0 96.1 jit_solution(15606150463807987263)
XLA Ops:
  0.0 1.9 %collective-permute-start = (f32[2,512,128]{2,1,0:T(8,128)}, f32[2,512,128]{2,1,0:T(8,128)S(1)}, u32[]{:S(2)}, u32[]{:S(2)}) collective-permute-start(f32[2,512,128]{2,1,0:T(8,128)} %bitcast.19), channel_id=1, source_target_pairs={{0,128},{1,129},{2,130},{3,131},{4,132},{5,133},{6,134},{7,135},{8... | collective-permute-start | bytes 1572872 | tf_op jit(solution)/shard_map/ppermute | solution.py:220
  1.9 0.8 broadcast_in_dim.7
  2.7 0.1 broadcast_in_dim.8.unit_ref
  2.8 0.0 copy-start
  2.8 1.0 %copy-done = f32[2,4,128,128]{3,2,1,0:T(8,128)S(1)} copy-done((f32[2,4,128,128]{3,2,1,0:T(8,128)S(1)}, f32[2,4,128,128]{3,2,1,0:T(8,128)}, u32[]{:S(2)}) %copy-start) | copy-done | bytes 524312
  3.8 0.1 shard_map.64.own_ref
  3.9 0.1 collective-permute-done.other_ref
  4.0 0.1 shard_map.65
  4.1 33.9 %all_to_all.20 = f32[16,64,128]{2,1,0:T(8,128)S(1)} all-to-all(f32[16,64,128]{2,1,0:T(8,128)S(1)} %bitcast.15), channel_id=1, replica_groups={{0,4,8,12,16,20,24,28,256,260,264,268,272,276,280,284},{1,5,9,13,17,21,..., dimensions={0} | all-to-all | bytes 1048576 | tf_op jit(solution)/shard_map/all_to_all | solution.py:208
  38.1 0.9 copy.7
  39.0 0.0 copy-start.1
  39.0 0.0 copy-start.2
  39.0 7.3 %all-to-all-start.1 = ((f32[16,64,128]{2,1,0:T(8,128)}), f32[16,64,128]{2,1,0:T(8,128)S(1)}, u32[]{:S(2)}, u32[]{:S(2)}) async-start(f32[16,64,128]{2,1,0:T(8,128)} %bitcast.4), calls=%async_computation.1 | async-start | bytes 1048576 | tf_op jit(solution)/shard_map/all_to_all | solution.py:210
  46.4 0.0 copy-start.3
  46.4 0.0 copy-start.4
  46.4 0.0 copy-done.1
  46.4 0.0 copy-done.2
  46.4 0.6 copy-done.3
  47.0 0.0 copy-done.4
  47.1 1.6 %shard_map.66 = (bf16[2,512,512]{2,1,0:T(8,128)(2,1)S(1)}, bf16[2,256,256]{2,1,0:T(8,128)(2,1)S(1)}) custom-call(s32[2,7]{1,0:T(2,128)S(1)} %copy-done.3, s32[1,7]{1,0:T(1,128)S(1)} %bitcast.21, f32[16,128]{1,0:T(8,128)S(1)} %broadcast_in_dim.8.unit_ref, f32[2,2,128,128]{3,2,1,0:T(8,128)S(1)} %copy-done.1, f32[2,128,128]{2,1,0:T(8,128)S(1)} %copy-done.2), custom_call_target="tpu_custom_call" | custom-call | tf_op jit(solution)/shard_map/pallas_call | solution.py:197
  48.6 7.1 %all-to-all-done.1 = f32[16,64,128]{2,1,0:T(8,128)S(1)} async-done(((f32[16,64,128]{2,1,0:T(8,128)}), f32[16,64,128]{2,1,0:T(8,128)S(1)}, u32[]{:S(2)}, u32[]{:S(2)}) %all-to-all-start.1) | async-done | bytes 524320 | tf_op jit(solution)/shard_map/all_to_all | solution.py:210
  55.8 1.2 %shard_map.67 = f32[1024,128]{1,0:T(8,128)S(1)} custom-call(f32[1024,128]{1,0:T(8,128)S(1)} %bitcast.17, bf16[2,512,512]{2,1,0:T(8,128)(2,1)S(1)} %get-tuple-element.7.mid_ref, bf16[2,256,256]{2,1,0:T(8,128)(2,1)S(1)} %get-tuple-element.8.low_ref), custom_call_target="tpu_custom_call" | custom-call | tf_op jit(solution)/shard_map/pallas_call | solution.py:197
  57.0 13.0 %all_to_all.21 = f32[16,64,128]{2,1,0:T(8,128)S(1)} all-to-all(f32[16,64,128]{2,1,0:T(8,128)S(1)} %bitcast.18), channel_id=1, replica_groups={{0,1,2,3,35,34,33,32,64,65,66,67,99,98,97,96},{4,5,6,7,39,38,37,36,68,6..., dimensions={0} | all-to-all | bytes 1048576 | tf_op jit(solution)/shard_map/all_to_all | solution.py:208
  70.0 0.1 copy.8
  70.1 25.2 %all_to_all.22 = f32[16,64,128]{2,1,0:T(8,128)S(1)} all-to-all(f32[16,64,128]{2,1,0:T(8,128)S(1)} %bitcast.24), channel_id=1, replica_groups={{0,4,8,12,16,20,24,28,256,260,264,268,272,276,280,284},{1,5,9,13,17,21,..., dimensions={0} | all-to-all | bytes 1048576 | tf_op jit(solution)/shard_map/all_to_all | solution.py:210
  95.3 0.8 shard_map.68
Async XLA Ops:
  0.0 4.0 %collective-permute-start = (f32[2,512,128]{2,1,0:T(8,128)}, f32[2,512,128]{2,1,0:T(8,128)S(1)}, u32[]{:S(2)}, u32[]{:S(2)}) collective-permute-start(f32[2,512,128]{2,1,0:T(8,128)} %bitcast.19), channel_id=1, source_target_pairs={{0,128},{1,129},{2,130},{3,131},{4,132},{5,133},{6,134},{7,135},{8... | collective-permute-start | bytes 1572872 | tf_op jit(solution)/shard_map/ppermute | solution.py:220
  2.8 1.0 %copy-start = (f32[2,4,128,128]{3,2,1,0:T(8,128)S(1)}, f32[2,4,128,128]{3,2,1,0:T(8,128)}, u32[]{:S(2)}) copy-start(f32[2,4,128,128]{3,2,1,0:T(8,128)} %param.6) | copy-start | bytes 1572868
  39.0 7.4 %copy-start.1 = (f32[2,2,128,128]{3,2,1,0:T(8,128)S(1)}, f32[2,2,128,128]{3,2,1,0:T(8,128)}, u32[]{:S(2)}) copy-start(f32[2,2,128,128]{3,2,1,0:T(8,128)} %low_gates_ref.1) | copy-start | bytes 786436
  39.0 7.4 %copy-start.2 = (f32[2,128,128]{2,1,0:T(8,128)S(1)}, f32[2,128,128]{2,1,0:T(8,128)}, u32[]{:S(2)}) copy-start(f32[2,128,128]{2,1,0:T(8,128)} %mid_gate_ref.1) | copy-start | bytes 393220
  39.0 16.7 %all-to-all-start.1 = ((f32[16,64,128]{2,1,0:T(8,128)}), f32[16,64,128]{2,1,0:T(8,128)S(1)}, u32[]{:S(2)}, u32[]{:S(2)}) async-start(f32[16,64,128]{2,1,0:T(8,128)} %bitcast.4), calls=%async_computation.1 | async-start | bytes 1048576 | tf_op jit(solution)/shard_map/all_to_all | solution.py:210
  46.4 0.7 copy-start.3
  46.4 0.7 copy-start.4

commit v9 on v7

--- a/solution.py
+++ b/solution.py
@@ -10,10 +10,10 @@
 AXIS = "device"
 NUMBERS = np.arange(512).reshape(2, 2, 4, 8, 4).transpose(1, 0, 3, 2, 4).reshape(2, 16, 16)
 LINES = [[group.tolist() for group in NUMBERS[core].T] for core in range(2)]
-PLACES = [k ^ k >> 2 for k in range(16)]
+PLACES = [k ^ (k >> 2 & 1) * 3 for k in range(16)]
 PLANES = [[group[PLACES].tolist() for group in NUMBERS[core]] for core in range(2)]
 STAGES = (LINES[0] + PLANES[1], PLANES[0] + LINES[1])
-REPEATS = 13
+REPEATS = 26
 IN_VMEM = pl.BlockSpec(memory_space=pltpu.VMEM)
 
 
@@ -78,7 +78,7 @@
 
     def parts(number):
         plane = jnp.where(lines, number >> 4, number & 15)
-        plane = plane ^ plane >> 2
+        plane = plane ^ (plane >> 2 & 1) * 3
         line = jnp.where(lines, number & 15, number >> 4)
         return line >> 3, (plane >> 2) << 5 | (line & 7) << 2 | plane & 3
 
@@ -209,12 +209,13 @@
     )(*operands)
 
 
-def exchange(rows, stages):
+def exchange(rows, stages, beside=()):
     blocks = rows.reshape(16, 64, -1)
     blocks = lax.all_to_all(blocks, AXIS, 0, 0, axis_index_groups=stages[0], tiled=True)
+    blocks, beside = lax.optimization_barrier((blocks, beside))
     blocks = blocks.reshape(16, 16, 4, -1).transpose(1, 0, 2, 3).reshape(16, 64, -1)
     blocks = lax.all_to_all(blocks, AXIS, 0, 0, axis_index_groups=stages[1], tiled=True)
-    return blocks.reshape(rows.shape)
+    return blocks.reshape(rows.shape), beside
 
 
 def body(state, low_gates, low_order, high_gates, mid_gate, mid_order):
@@ -226,6 +227,10 @@
     other = lax.ppermute(mine, AXIS, [(number, number ^ 128) for number in range(512)])
     units = jnp.broadcast_to(high_gates.reshape(16, 1), (16, order))
     own = call(own_kernel, rows, units, mine)
+    sent = call(first_kernel, rows, units, own, other)
+    sent, low_gates, low_order, mid_gate, mid_order = lax.optimization_barrier(
+        (sent, low_gates, low_order, mid_gate, mid_order)
+    )
     mid, low = call(
         gates_kernel,
         [
@@ -238,10 +243,9 @@
         low_gates,
         mid_gate,
     )
-    sent = call(first_kernel, rows, units, own, other)
-    moved = exchange(sent, STAGES)
+    moved, (mid, low) = exchange(sent, STAGES, (mid, low))
     done = call(middle_kernel, rows, moved, mid, low)
-    back = exchange(done, STAGES[::-1])
+    back, _ = exchange(done, STAGES[::-1])
     final = jax.ShapeDtypeStruct(mine.shape, jnp.float32)
     return call(last_kernel, final, back).reshape(state.shape)
 

time: 96.6 us -> 96.6 us (level)
  blocking collectives: 71.9 us -> 54.6 us
  waiting for transfers between devices: 7.46 us -> 16.8 us
  starting transfers between devices: 9.37 us -> 17.3 us
    all_to_all x2 -> x1, blocking collectives: 46.9 us -> 13 us  [exchange(): lax.all_to_all(blocks, AXIS, 0, 0, axis_index_groups=stages[0], tiled=True)]
    all_to_all x1 -> x2, blocking collectives: 25 us -> 41.7 us  [exchange(): lax.all_to_all(blocks, AXIS, 0, 0, axis_index_groups=stages[1], tiled=True)]
    all_to_all x1, waiting for transfers between devices: 7.34 us -> 16.7 us  [exchange(): lax.all_to_all(blocks, AXIS, 0, 0, axis_index_groups=stages[0], tiled=True)]
    all_to_all x1, starting transfers between devices: 7.46 us -> 15.3 us  [exchange(): lax.all_to_all(blocks, AXIS, 0, 0, axis_index_groups=stages[0], tiled=True)]
where the time goes in v9:
time: 96.6 us; the launch traced here: 96.1 us
  blocking collectives  54.6 us (57%)
  starting transfers between devices  17.3 us (18%)
  waiting for transfers between devices  16.8 us (17%)
  Pallas kernels  4.59 us (5%)
  local copies, waits for them, and re-layouts  2.8 us (3%)
    all_to_all x2, blocking collectives, exchange(): lax.all_to_all(blocks, AXIS, 0, 0, axis_index_groups=stages[1], tiled=True)  41.7 us
    all_to_all x1, waiting for transfers between devices, exchange(): lax.all_to_all(blocks, AXIS, 0, 0, axis_index_groups=stages[0], tiled=True)  16.7 us
    all_to_all x1, starting transfers between devices, exchange(): lax.all_to_all(blocks, AXIS, 0, 0, axis_index_groups=stages[0], tiled=True)  15.3 us
    all_to_all x1, blocking collectives, exchange(): lax.all_to_all(blocks, AXIS, 0, 0, axis_index_groups=stages[0], tiled=True)  13 us
    pallas_call x5, Pallas kernels, call(): pl.pallas_call(kernel, out_shape=out, in_specs=[IN_VMEM] * len(operands),...  4.59 us
  transfers between devices with their start and end apart: 2, of which 2 were waited for; matrix products, arithmetic and copies ran while one was open for 1% of the time, Pallas kernels for 2%

profile of v9, /device:TPU:32, one launch (start us, length us, event | category | flops | bytes accessed | tf_op | source)
XLA Modules:
  0.0 96.1 jit_solution(10384164644183570042)
XLA Ops:
  0.0 1.9 %collective-permute-start = (f32[2,512,128]{2,1,0:T(8,128)}, f32[2,512,128]{2,1,0:T(8,128)S(1)}, u32[]{:S(2)}, u32[]{:S(2)}) collective-permute-start(f32[2,512,128]{2,1,0:T(8,128)} %bitcast.18), channel_id=1, source_target_pairs={{0,128},{1,129},{2,130},{3,131},{4,132},{5,133},{6,134},{7,135},{8... | collective-permute-start | bytes 1572872 | tf_op jit(solution)/shard_map/ppermute | solution.py:227
  1.9 0.8 broadcast_in_dim.7
  2.7 0.1 broadcast_in_dim.8.unit_ref
  2.8 0.0 copy-start
  2.8 1.0 %copy-done = f32[2,4,128,128]{3,2,1,0:T(8,128)S(1)} copy-done((f32[2,4,128,128]{3,2,1,0:T(8,128)S(1)}, f32[2,4,128,128]{3,2,1,0:T(8,128)}, u32[]{:S(2)}) %copy-start) | copy-done | bytes 524312
  3.8 0.1 shard_map.64.own_ref
  3.9 0.1 collective-permute-done.other_ref
  4.0 0.9 shard_map.65
  4.9 0.0 copy-start.1
  4.9 0.0 copy-start.2
  4.9 15.3 %all-to-all-start = ((f32[16,64,128]{2,1,0:T(8,128)}), f32[16,64,128]{2,1,0:T(8,128)S(1)}, u32[]{:S(2)}, u32[]{:S(2)}) async-start(f32[16,64,128]{2,1,0:T(8,128)} %bitcast.1), calls=%async_computation | async-start | bytes 1048576 | tf_op jit(solution)/shard_map/all_to_all | solution.py:214
  20.3 0.0 copy-start.3
  20.3 0.0 copy-start.4
  20.3 0.0 copy-done.1
  20.3 0.0 copy-done.2
  20.3 0.6 copy-done.3
  20.9 0.0 copy-done.4
  20.9 1.6 %shard_map.66 = (bf16[2,512,512]{2,1,0:T(8,128)(2,1)S(1)}, bf16[2,256,256]{2,1,0:T(8,128)(2,1)S(1)}) custom-call(s32[2,7]{1,0:T(2,128)S(1)} %copy-done.3, s32[1,7]{1,0:T(1,128)S(1)} %bitcast.20, f32[16,128]{1,0:T(8,128)S(1)} %broadcast_in_dim.8.unit_ref, f32[2,2,128,128]{3,2,1,0:T(8,128)S(1)} %copy-done.1, f32[2,128,128]{2,1,0:T(8,128)S(1)} %copy-done.2), custom_call_target="tpu_custom_call" | custom-call | tf_op jit(solution)/shard_map/pallas_call | solution.py:203
  22.5 16.7 %all-to-all-done = f32[16,64,128]{2,1,0:T(8,128)S(1)} async-done(((f32[16,64,128]{2,1,0:T(8,128)}), f32[16,64,128]{2,1,0:T(8,128)S(1)}, u32[]{:S(2)}, u32[]{:S(2)}) %all-to-all-start) | async-done | bytes 524320 | tf_op jit(solution)/shard_map/all_to_all | solution.py:214
  39.2 0.1 copy.7
  39.3 16.5 %all_to_all.20 = f32[16,64,128]{2,1,0:T(8,128)S(1)} all-to-all(f32[16,64,128]{2,1,0:T(8,128)S(1)} %bitcast.22), channel_id=1, replica_groups={{0,1,2,3,35,34,33,32,64,65,66,67,99,98,97,96},{4,5,6,7,39,38,37,36,68,6..., dimensions={0} | all-to-all | bytes 1048576 | tf_op jit(solution)/shard_map/all_to_all | solution.py:217
  55.8 1.2 %shard_map.67 = f32[1024,128]{1,0:T(8,128)S(1)} custom-call(f32[1024,128]{1,0:T(8,128)S(1)} %bitcast.16, bf16[2,512,512]{2,1,0:T(8,128)(2,1)S(1)} %get-tuple-element.23.mid_ref, bf16[2,256,256]{2,1,0:T(8,128)(2,1)S(1)} %get-tuple-element.24.low_ref), custom_call_target="tpu_custom_call" | custom-call | tf_op jit(solution)/shard_map/pallas_call | solution.py:203
  57.0 13.0 %all_to_all.21 = f32[16,64,128]{2,1,0:T(8,128)S(1)} all-to-all(f32[16,64,128]{2,1,0:T(8,128)S(1)} %bitcast.17), channel_id=1, replica_groups={{0,1,2,3,35,34,33,32,64,65,66,67,99,98,97,96},{4,5,6,7,39,38,37,36,68,6..., dimensions={0} | all-to-all | bytes 1048576 | tf_op jit(solution)/shard_map/all_to_all | solution.py:214
  70.0 0.1 copy.8
  70.2 25.1 %all_to_all.22 = f32[16,64,128]{2,1,0:T(8,128)S(1)} all-to-all(f32[16,64,128]{2,1,0:T(8,128)S(1)} %bitcast.24), channel_id=1, replica_groups={{0,4,8,12,16,20,24,28,256,260,264,268,272,276,280,284},{1,5,9,13,17,21,..., dimensions={0} | all-to-all | bytes 1048576 | tf_op jit(solution)/shard_map/all_to_all | solution.py:217
  95.3 0.8 shard_map.68
Async XLA Ops:
  0.0 4.0 %collective-permute-start = (f32[2,512,128]{2,1,0:T(8,128)}, f32[2,512,128]{2,1,0:T(8,128)S(1)}, u32[]{:S(2)}, u32[]{:S(2)}) collective-permute-start(f32[2,512,128]{2,1,0:T(8,128)} %bitcast.18), channel_id=1, source_target_pairs={{0,128},{1,129},{2,130},{3,131},{4,132},{5,133},{6,134},{7,135},{8... | collective-permute-start | bytes 1572872 | tf_op jit(solution)/shard_map/ppermute | solution.py:227
  2.8 1.0 %copy-start = (f32[2,4,128,128]{3,2,1,0:T(8,128)S(1)}, f32[2,4,128,128]{3,2,1,0:T(8,128)}, u32[]{:S(2)}) copy-start(f32[2,4,128,128]{3,2,1,0:T(8,128)} %param.6) | copy-start | bytes 1572868
  4.9 15.4 %copy-start.1 = (f32[2,2,128,128]{3,2,1,0:T(8,128)S(1)}, f32[2,2,128,128]{3,2,1,0:T(8,128)}, u32[]{:S(2)}) copy-start(f32[2,2,128,128]{3,2,1,0:T(8,128)} %low_gates_ref) | copy-start | bytes 786436
  4.9 15.4 %copy-start.2 = (f32[2,128,128]{2,1,0:T(8,128)S(1)}, f32[2,128,128]{2,1,0:T(8,128)}, u32[]{:S(2)}) copy-start(f32[2,128,128]{2,1,0:T(8,128)} %mid_gate_ref) | copy-start | bytes 393220
  4.9 34.2 %all-to-all-start = ((f32[16,64,128]{2,1,0:T(8,128)}), f32[16,64,128]{2,1,0:T(8,128)S(1)}, u32[]{:S(2)}, u32[]{:S(2)}) async-start(f32[16,64,128]{2,1,0:T(8,128)} %bitcast.1), calls=%async_computation | async-start | bytes 1048576 | tf_op jit(solution)/shard_map/all_to_all | solution.py:214
  20.3 0.7 copy-start.3
  20.3 0.7 copy-start.4

commit v10 on v9

--- a/solution.py
+++ b/solution.py
@@ -13,7 +13,7 @@
 PLACES = [k ^ (k >> 2 & 1) * 3 for k in range(16)]
 PLANES = [[group[PLACES].tolist() for group in NUMBERS[core]] for core in range(2)]
 STAGES = (LINES[0] + PLANES[1], PLANES[0] + LINES[1])
-REPEATS = 26
+REPEATS = 20
 IN_VMEM = pl.BlockSpec(memory_space=pltpu.VMEM)
 
 

time: 96.6 us -> 96.4 us (level)
  no operation moved by 1% of the time
where the time goes in v10:
time: 96.4 us; the launch traced here: 96 us
  blocking collectives  54.5 us (57%)
  starting transfers between devices  17.3 us (18%)
  waiting for transfers between devices  16.8 us (17%)
  Pallas kernels  4.59 us (5%)
  local copies, waits for them, and re-layouts  2.8 us (3%)
    all_to_all x2, blocking collectives, exchange(): lax.all_to_all(blocks, AXIS, 0, 0, axis_index_groups=stages[1], tiled=True)  41.5 us
    all_to_all x1, waiting for transfers between devices, exchange(): lax.all_to_all(blocks, AXIS, 0, 0, axis_index_groups=stages[0], tiled=True)  16.7 us
    all_to_all x1, starting transfers between devices, exchange(): lax.all_to_all(blocks, AXIS, 0, 0, axis_index_groups=stages[0], tiled=True)  15.3 us
    all_to_all x1, blocking collectives, exchange(): lax.all_to_all(blocks, AXIS, 0, 0, axis_index_groups=stages[0], tiled=True)  13 us
    pallas_call x5, Pallas kernels, call(): pl.pallas_call(kernel, out_shape=out, in_specs=[IN_VMEM] * len(operands),...  4.59 us
  transfers between devices with their start and end apart: 2, of which 2 were waited for; matrix products, arithmetic and copies ran while one was open for 1% of the time, Pallas kernels for 2%

profile of v10, /device:TPU:32, one launch (start us, length us, event | category | flops | bytes accessed | tf_op | source)
XLA Modules:
  0.0 96.0 jit_solution(17149605847703671519)
XLA Ops:
  0.0 1.9 %collective-permute-start = (f32[2,512,128]{2,1,0:T(8,128)}, f32[2,512,128]{2,1,0:T(8,128)S(1)}, u32[]{:S(2)}, u32[]{:S(2)}) collective-permute-start(f32[2,512,128]{2,1,0:T(8,128)} %bitcast.18), channel_id=1, source_target_pairs={{0,128},{1,129},{2,130},{3,131},{4,132},{5,133},{6,134},{7,135},{8... | collective-permute-start | bytes 1572872 | tf_op jit(solution)/shard_map/ppermute | solution.py:227
  1.9 0.8 broadcast_in_dim.7
  2.7 0.1 broadcast_in_dim.8.unit_ref
  2.8 0.0 copy-start
  2.8 1.0 %copy-done = f32[2,4,128,128]{3,2,1,0:T(8,128)S(1)} copy-done((f32[2,4,128,128]{3,2,1,0:T(8,128)S(1)}, f32[2,4,128,128]{3,2,1,0:T(8,128)}, u32[]{:S(2)}) %copy-start) | copy-done | bytes 524312
  3.8 0.1 shard_map.64.own_ref
  3.9 0.1 collective-permute-done.other_ref
  4.0 0.9 shard_map.65
  4.9 0.0 copy-start.1
  4.9 0.0 copy-start.2
  4.9 15.3 %all-to-all-start = ((f32[16,64,128]{2,1,0:T(8,128)}), f32[16,64,128]{2,1,0:T(8,128)S(1)}, u32[]{:S(2)}, u32[]{:S(2)}) async-start(f32[16,64,128]{2,1,0:T(8,128)} %bitcast.1), calls=%async_computation | async-start | bytes 1048576 | tf_op jit(solution)/shard_map/all_to_all | solution.py:214
  20.3 0.0 copy-start.3
  20.3 0.0 copy-start.4
  20.3 0.0 copy-done.1
  20.3 0.0 copy-done.2
  20.3 0.6 copy-done.3
  20.9 0.0 copy-done.4
  20.9 1.6 %shard_map.66 = (bf16[2,512,512]{2,1,0:T(8,128)(2,1)S(1)}, bf16[2,256,256]{2,1,0:T(8,128)(2,1)S(1)}) custom-call(s32[2,7]{1,0:T(2,128)S(1)} %copy-done.3, s32[1,7]{1,0:T(1,128)S(1)} %bitcast.20, f32[16,128]{1,0:T(8,128)S(1)} %broadcast_in_dim.8.unit_ref, f32[2,2,128,128]{3,2,1,0:T(8,128)S(1)} %copy-done.1, f32[2,128,128]{2,1,0:T(8,128)S(1)} %copy-done.2), custom_call_target="tpu_custom_call" | custom-call | tf_op jit(solution)/shard_map/pallas_call | solution.py:203
  22.5 16.7 %all-to-all-done = f32[16,64,128]{2,1,0:T(8,128)S(1)} async-done(((f32[16,64,128]{2,1,0:T(8,128)}), f32[16,64,128]{2,1,0:T(8,128)S(1)}, u32[]{:S(2)}, u32[]{:S(2)}) %all-to-all-start) | async-done | bytes 524320 | tf_op jit(solution)/shard_map/all_to_all | solution.py:214
  39.2 0.1 copy.7
  39.3 16.3 %all_to_all.20 = f32[16,64,128]{2,1,0:T(8,128)S(1)} all-to-all(f32[16,64,128]{2,1,0:T(8,128)S(1)} %bitcast.22), channel_id=1, replica_groups={{0,1,2,3,35,34,33,32,64,65,66,67,99,98,97,96},{4,5,6,7,39,38,37,36,68,6..., dimensions={0} | all-to-all | bytes 1048576 | tf_op jit(solution)/shard_map/all_to_all | solution.py:217
  55.6 1.2 %shard_map.67 = f32[1024,128]{1,0:T(8,128)S(1)} custom-call(f32[1024,128]{1,0:T(8,128)S(1)} %bitcast.16, bf16[2,512,512]{2,1,0:T(8,128)(2,1)S(1)} %get-tuple-element.23.mid_ref, bf16[2,256,256]{2,1,0:T(8,128)(2,1)S(1)} %get-tuple-element.24.low_ref), custom_call_target="tpu_custom_call" | custom-call | tf_op jit(solution)/shard_map/pallas_call | solution.py:203
  56.8 13.0 %all_to_all.21 = f32[16,64,128]{2,1,0:T(8,128)S(1)} all-to-all(f32[16,64,128]{2,1,0:T(8,128)S(1)} %bitcast.17), channel_id=1, replica_groups={{0,1,2,3,35,34,33,32,64,65,66,67,99,98,97,96},{4,5,6,7,39,38,37,36,68,6..., dimensions={0} | all-to-all | bytes 1048576 | tf_op jit(solution)/shard_map/all_to_all | solution.py:214
  69.8 0.1 copy.8
  70.0 25.2 %all_to_all.22 = f32[16,64,128]{2,1,0:T(8,128)S(1)} all-to-all(f32[16,64,128]{2,1,0:T(8,128)S(1)} %bitcast.24), channel_id=1, replica_groups={{0,4,8,12,16,20,24,28,256,260,264,268,272,276,280,284},{1,5,9,13,17,21,..., dimensions={0} | all-to-all | bytes 1048576 | tf_op jit(solution)/shard_map/all_to_all | solution.py:217
  95.1 0.8 shard_map.68
Async XLA Ops:
  0.0 4.0 %collective-permute-start = (f32[2,512,128]{2,1,0:T(8,128)}, f32[2,512,128]{2,1,0:T(8,128)S(1)}, u32[]{:S(2)}, u32[]{:S(2)}) collective-permute-start(f32[2,512,128]{2,1,0:T(8,128)} %bitcast.18), channel_id=1, source_target_pairs={{0,128},{1,129},{2,130},{3,131},{4,132},{5,133},{6,134},{7,135},{8... | collective-permute-start | bytes 1572872 | tf_op jit(solution)/shard_map/ppermute | solution.py:227
  2.8 1.0 %copy-start = (f32[2,4,128,128]{3,2,1,0:T(8,128)S(1)}, f32[2,4,128,128]{3,2,1,0:T(8,128)}, u32[]{:S(2)}) copy-start(f32[2,4,128,128]{3,2,1,0:T(8,128)} %param.6) | copy-start | bytes 1572868
  4.9 15.4 %copy-start.1 = (f32[2,2,128,128]{3,2,1,0:T(8,128)S(1)}, f32[2,2,128,128]{3,2,1,0:T(8,128)}, u32[]{:S(2)}) copy-start(f32[2,2,128,128]{3,2,1,0:T(8,128)} %low_gates_ref) | copy-start | bytes 786436
  4.9 15.4 %copy-start.2 = (f32[2,128,128]{2,1,0:T(8,128)S(1)}, f32[2,128,128]{2,1,0:T(8,128)}, u32[]{:S(2)}) copy-start(f32[2,128,128]{2,1,0:T(8,128)} %mid_gate_ref) | copy-start | bytes 393220
  4.9 34.2 %all-to-all-start = ((f32[16,64,128]{2,1,0:T(8,128)}), f32[16,64,128]{2,1,0:T(8,128)S(1)}, u32[]{:S(2)}, u32[]{:S(2)}) async-start(f32[16,64,128]{2,1,0:T(8,128)} %bitcast.1), calls=%async_computation | async-start | bytes 1048576 | tf_op jit(solution)/shard_map/all_to_all | solution.py:214
  20.3 0.7 copy-start.3
  20.3 0.7 copy-start.4
